TPU v7x, 32 devices: a whole 2x2x4 slice. The times are simulated.
32 devices in a mesh: groups: 2 (over y), seq: 4 (over z), tp: 2 (over x), kvh: 2 (over core).
Axes of the slice: x: 2, y: 2, z: 4, core: 2. Of those that a mesh axis runs over, the one named last changes fastest.
Arguments:
- pool_kv: bfloat16 [16, 2, 256, 512], P(('groups', 'seq'), None, None, ('tp', 'kvh')), parts along dimension 0, may hold values from -24 to 24
- hidden_rows: bfloat16 [16, 40, 4096], P(('groups', 'seq'), None, ('tp', 'kvh')), parts along dimension 0, may hold values from -512 to 512
- norm_gain: bfloat16 [4096], P(('tp', 'kvh')), may hold values from 0.099609375 to 1.8984375
- kv_weight: bfloat16 [4096, 1024], P(('tp', 'kvh')), may hold values from -0.09375 to 0.09375
- queries: bfloat16 [16, 40, 4096], P(('groups', 'seq'), None, ('tp', 'kvh')), parts along dimension 0, may hold values from -64 to 64
- stretch_slot: int32 [8], P('groups'), parts along dimension 0, may hold values from 0 to 7, as said below
- stretch_lengths: int32 [8], P('groups'), parts along dimension 0, may hold values from 128 to 256
- recompute_rows: int32 [16, 40], P(('groups', 'seq')), parts along dimension 0, may hold values from 0 to 255, as said below
Outputs:
- fresh_kv: bfloat16 [16, 2, 40, 512], P(('groups', 'seq'), None, None, ('tp', 'kvh')), parts along dimension 0
- attended: bfloat16 [16, 40, 4096], P(('groups', 'seq'), None, ('tp', 'kvh')), parts along dimension 0
There are 2 independent parts, one for each index of `groups`. A program takes and returns all parts, laid end to end along the dimension named above; an argument that names none is the same for every part. Nothing has to cross between parts.
Inputs may be any that keep to these rules, and one draw needn't show every extreme that they name: `stretch_slot`: distinct pool slots; slot s lies with owner s // 2 along seq. `recompute_rows`: each row distinct and ascending, below the length of the stretch that the slot holds, and below 128 in a slot that holds none.
All inputs are finite; a program needn't handle non-finite values.
Results may differ from a plain program's by a relative error of at most 0.011.
Values may be sent and summed in bfloat16 or wider, within the bound.
No kernel may reach another device: no remote copies, remote signals or barrier semaphores. Data moves between devices by JAX's collectives and lax.ppermute only.
A program may use at most 128 MiB of HBM per device.

v0:
```python
import jax
import jax.numpy as jnp
from jax import lax
from jax.sharding import PartitionSpec as P

D = 4096


THETA = 500000.0


def rotate(values, positions):
    half = values.shape[-1] // 2
    inverse = THETA ** (-(jnp.arange(half, dtype=jnp.float32) * 2.0) / values.shape[-1])
    angle = positions.astype(jnp.float32)[..., None] * inverse
    cosine = jnp.cos(angle)
    sine = jnp.sin(angle)
    first = values[..., :half]
    second = values[..., half:]
    return jnp.concatenate([first * cosine - second * sine, second * cosine + first * sine], -1)


def absorb(state_now, query_mat, query_pos, key_rows, value_rows, key_pos, key_valid, scale):
    run_max, run_sum, run_acc = state_now
    scores = (
        jnp.einsum("qh,kh->qk", query_mat, key_rows, preferred_element_type=jnp.float32) * scale
    )
    visible = key_valid[None, :] & (key_pos[None, :] <= query_pos[:, None])
    masked = jnp.where(visible, scores, -1e30)
    new_max = jnp.maximum(run_max, jnp.max(masked, 1))
    weight = jnp.where(visible, jnp.exp(masked - new_max[:, None]), 0.0)
    new_sum = jnp.sum(weight, 1)
    new_acc = jnp.dot(weight.astype(jnp.bfloat16), value_rows, preferred_element_type=jnp.float32)
    return (new_max, new_sum, new_acc)


def empty_state(count, width):
    return (
        jnp.full((count,), -1e30, jnp.float32),
        jnp.zeros((count,), jnp.float32),
        jnp.zeros((count, width), jnp.float32),
    )


def local(
    pool_kv,
    hidden_rows,
    norm_gain,
    kv_weight,
    queries,
    stretch_slot,
    stretch_lengths,
    recompute_rows,
):
    slot_count = pool_kv.shape[0]
    span = pool_kv.shape[2]
    width = pool_kv.shape[3]
    row_count = recompute_rows.shape[1]
    group = queries.shape[2] // width
    seq_count = lax.axis_size("seq")
    seq_index = lax.axis_index("seq")
    stretch_count = stretch_slot.shape[0]
    scale = width ** (-0.5)
    inputs = hidden_rows.astype(jnp.float32)
    squares = lax.psum(jnp.sum(inputs * inputs, -1), ("tp", "kvh"))
    inverse_rms = lax.rsqrt(squares / D + 1e-05)
    normed = (inputs * inverse_rms[..., None] * norm_gain.astype(jnp.float32)).astype(jnp.bfloat16)
    normed = normed.reshape(slot_count * row_count, -1)
    product = jnp.dot(normed, kv_weight, preferred_element_type=jnp.float32)
    mine = lax.psum_scatter(
        product.reshape(slot_count * row_count, 1 * lax.axis_size(("tp", "kvh")), 2 * width)
        .transpose(1, 0, 2)
        .astype(jnp.bfloat16),
        ("tp", "kvh"),
        scatter_dimension=0,
        tiled=True,
    ).astype(jnp.float32)
    fresh_kv = (
        mine[0].astype(jnp.bfloat16).reshape(slot_count, row_count, 2, width).transpose(0, 2, 1, 3)
    )
    token_ids = jnp.arange(span, dtype=jnp.int32)
    onehot = recompute_rows[:, :, None] == token_ids[None, None, :]
    placed = jnp.einsum(
        "src,strh->stch", onehot.astype(jnp.bfloat16), fresh_kv, preferred_element_type=jnp.float32
    ).astype(jnp.bfloat16)
    replaced = jnp.any(onehot, 1)
    patched = jnp.where(replaced[:, None, :, None], placed, pool_kv)
    global_slots = seq_index * slot_count + jnp.arange(slot_count, dtype=jnp.int32)
    position_ids = jnp.arange(stretch_count, dtype=jnp.int32)
    hits = stretch_slot[:, None] == global_slots[None, :]
    my_held = jnp.any(hits, 0)
    my_pos = jnp.where(my_held, jnp.sum(jnp.where(hits, position_ids[:, None], 0), 0), -1)
    pool_ids = jnp.arange(slot_count * seq_count, dtype=jnp.int32)
    pool_hits = stretch_slot[:, None] == pool_ids[None, :]
    pool_held = jnp.any(pool_hits, 0)
    pool_pos = jnp.where(pool_held, jnp.sum(jnp.where(pool_hits, position_ids[:, None], 0), 0), -1)
    pool_len = jnp.sum(jnp.where(pool_hits, stretch_lengths[:, None], 0), 0)
    key_pos_mine = my_pos[:, None] * span + token_ids[None, :]
    rotated_keys = rotate(patched[:, 0].astype(jnp.float32), key_pos_mine).astype(jnp.bfloat16)
    kv_rot = jnp.stack([rotated_keys, patched[:, 1]], 1)
    query_pos = my_pos[:, None] * span + recompute_rows
    query_four = queries.reshape(slot_count, row_count, group, width).astype(jnp.float32)
    rotated_queries = rotate(query_four, query_pos[:, :, None]).astype(jnp.bfloat16)
    query_mat = rotated_queries.reshape(slot_count * row_count * group, width)
    query_at = jnp.broadcast_to(query_pos[:, :, None], (slot_count, row_count, group)).reshape(
        slot_count * row_count * group
    )
    block_kv = lax.all_gather(kv_rot, "seq", axis=0, tiled=True)
    block_count = block_kv.shape[0]
    key_rows = block_kv[:, 0].reshape(block_count * span, width)
    value_rows = block_kv[:, 1].reshape(block_count * span, width)
    block_pos = pool_pos
    key_at = (block_pos[:, None] * span + token_ids[None, :]).reshape(block_count * span)
    key_valid = ((block_pos[:, None] >= 0) & (token_ids[None, :] < pool_len[:, None])).reshape(
        block_count * span
    )
    key_rows, value_rows, key_at, key_valid, block_pos = (
        key_rows,
        value_rows,
        key_at,
        key_valid,
        block_pos,
    )
    run_max, run_sum, run_acc = absorb(
        empty_state(slot_count * row_count * group, width),
        query_mat,
        query_at,
        key_rows,
        value_rows,
        key_at,
        key_valid,
        scale,
    )
    result = run_acc / jnp.where(run_sum > 0, run_sum, 1.0)[:, None]
    result = result.reshape(slot_count, row_count, group * width)
    attended = jnp.where(my_held[:, None, None], result, 0.0).astype(jnp.bfloat16)
    return (fresh_kv, attended)


def solution(mesh):
    in_specs = (
        P(("groups", "seq"), None, None, ("tp", "kvh")),
        P(("groups", "seq"), None, ("tp", "kvh")),
        P(("tp", "kvh")),
        P(("tp", "kvh"), None),
        P(("groups", "seq"), None, ("tp", "kvh")),
        P("groups"),
        P("groups"),
        P(("groups", "seq"), None),
    )
    out_specs = (
        P(("groups", "seq"), None, None, ("tp", "kvh")),
        P(("groups", "seq"), None, ("tp", "kvh")),
    )
    return jax.shard_map(local, mesh=mesh, in_specs=in_specs, out_specs=out_specs, check_vma=False)
```

profile of v0, /device:TPU:0, one launch (start us, length us, event | category | flops | bytes accessed | tf_op | source)
XLA Modules:
  0.0 88.6 jit_solution(16149561881759661497)
XLA Ops:
  7.2 1.1 %fusion.9 = f32[2,40]{1,0:T(2,128)S(1)} fusion(bf16[2,40,1024]{2,1,0:T(8,128)(2,1)} %param.9), kind=kLoop, calls=%fused_computation.14 | loop fusion | flops 245680 | bytes 164160 | tf_op jit(solution)/shard_map/reduce_sum | solution.py:65
  8.3 8.3 %psum.7 = f32[2,40]{1,0:T(2,128)S(1)} all-reduce(f32[2,40]{1,0:T(2,128)S(1)} %fusion.9), channel_id=1, replica_groups=mesh['groups'=2,'seq'=4,'tp'=2,'kvh'=2] {'tp','kvh'}, use_global_device_ids=true, to_apply=%region_1.0 | all-reduce | flops 80 | bytes 640 | tf_op jit(solution)/shard_map/psum | solution.py:65
  16.7 0.7 convert_element_type.68
  17.4 2.9 %copy.40 = bf16[1024,1024]{1,0:T(8,128)(2,1)S(1)} copy(bf16[1024,1024]{0,1:T(8,128)(2,1)} %bitcast.55) | data formatting | bytes 4194304 | tf_op jit(solution)/shard_map/dot_general | solution.py:69
  20.3 1.0 %fusion.11 = bf16[2,40,1024]{2,1,0:T(8,128)(2,1)S(1)} fusion(bf16[2,40,1024]{2,1,0:T(8,128)(2,1)} %param.9, f32[1024]{0:T(1024)S(1)} %convert_element_type.68, f32[2,40]{1,0:T(2,128)S(1)} %add_rsqrt_fusion), kind=kLoop, calls=%fused_computation.16 | loop fusion | flops 327680 | bytes 332096 | tf_op jit(solution)/shard_map/convert_element_type | solution.py:67
  21.3 1.4 %fusion.8 = bf16[4,80,256]{2,1,0:T(8,128)(2,1)} fusion(bf16[80,1024,1]{1,0,2:T(8,128)(2,1)S(1)} %bitcast.56, bf16[4,256,1024]{2,1,0:T(8,128)(2,1)S(1)} %bitcast.53), kind=kOutput, calls=%fused_computation.11 | convolution fusion | flops 167854080 | bytes 2424832 | tf_op jit(solution)/shard_map/dot_general | solution.py:69
  22.8 0.2 compare_reduce_fusion
  23.0 0.2 fusion.33
  23.3 0.1 fusion.26
  23.5 0.1 copy.33
  23.7 19.2 %reduce-scatter.2.cloned.1.call-done = bf16[1,80,256]{2,1,0:T(8,128)(2,1)} async-done(((bf16[4,80,256]{2,1,0:T(8,128)(2,1)}), bf16[1,80,256]{2,1,0:T(8,128)(2,1)}) %reduce-scatter.2.cloned.1.call-update) | async-done | bytes 40976 | tf_op jit(solution)/shard_map/reduce_scatter | solution.py:70
  42.9 0.8 convert_element_type.72
  43.7 0.3 fusion.7
  44.1 0.6 fusion.29
  44.7 0.9 copy.36
  45.9 0.1 le.16
  46.0 0.2 multiply_cosine_fusion.1
  46.3 0.2 subtract_convert_fusion
  46.5 27.2 %all-gather.2.cloned.1.call-done = bf16[8,2,256,128]{3,2,1,0:T(8,128)(2,1)} async-done(((bf16[2,2,256,128]{3,2,1,0:T(8,128)(2,1)}), bf16[8,2,256,128]{3,2,1,0:T(8,128)(2,1)}) %all-gather.2.cloned.1.call-update) | async-done | bytes 1048592 | tf_op jit(solution)/shard_map/all_gather | solution.py:108
  73.7 1.3 %fusion.37 = (bf16[8,1,256,128]{3,2,1,0:T(8,128)(2,1)S(1)}, bf16[8,1,256,128]{3,2,1,0:T(8,128)(2,1)S(1)}) fusion(bf16[8,2,256,128]{3,2,1,0:T(8,128)(2,1)} %all-gather.2.cloned.1.call-done), kind=kLoop, calls=%fused_computation.70 | loop fusion | bytes 2097152 | tf_op jit(solution)/shard_map/slice | solution.py:110
  74.9 1.6 %fusion = (f32[640]{0:T(1024)S(1)}, f32[640,2048]{1,0:T(8,128)S(1)}) fusion(s32[2048]{0:T(1024)S(1)} %bitcast.64, s32[640]{0:T(1024)S(1)} %le.16, pred[2048]{0:T(1024)(128)(4,1)S(1)} %and.26, bf16[2048,128]{1,0:T(8,128)(2,1)S(1)} %bitcast.58, bf16[640,64]{1,0:T(8,128)(2,1)S(1)} %bitcast.63, bf16[640,64]{1,0:T(8,128)(2,1)S(1)} %bitcast.62), kind=kOutput, calls=%fused_computation.3 | convolution fusion | flops 342424960 | bytes 5946368 | tf_op jit(solution)/shard_map/qh,kh->qk/dot_general | solution.py:26
  76.5 2.0 %fusion.35 = f32[640]{0:T(1024)S(1)} fusion(f32[640]{0:T(1024)S(1)} %broadcast_maximum_fusion, f32[640,2048]{1,0:T(8,128)S(1)} %get-tuple-element.17, s32[640]{0:T(1024)S(1)} %le.16, s32[2048]{0:T(1024)S(1)} %bitcast.65, pred[2048]{0:T(1024)(128)(4,1)S(1)} %and.26), kind=kLoop, calls=%fused_computation.68 | loop fusion | flops 9174400 | bytes 5260800 | tf_op jit(solution)/shard_map/reduce_sum | solution.py:32
  78.6 2.3 %fusion.3 = bf16[640,128]{1,0:T(8,128)(2,1)S(1)} fusion(bf16[2048,128]{1,0:T(8,128)(2,1)S(1)} %bitcast.57, f32[640]{0:T(1024)S(1)} %compare_select_fusion, f32[640,2048]{1,0:T(8,128)S(1)} %get-tuple-element.17, f32[640]{0:T(1024)S(1)} %broadcast_maximum_fusion, s32[2048]{0:T(1024)S(1)} %bitcast.66, s32[640]{0:T(1024)S(1)} %le.16, pred[2048]{0:T(1024)(128)(4,1)S(1)} %and.26), kind=kOutput, calls=%fused_computation.7 | convolution fusion | flops 344883200 | bytes 5948928 | tf_op jit(solution)/shard_map/dot_general | solution.py:33
  81.0 0.8 select_convert_fusion
  (38 shorter events, 0.9 us)
Async XLA Ops:
  7.2 15.6 %copy-start.4 = (s32[4]{0:T(128)S(1)}, s32[4]{0:T(128)}, u32[]{:S(2)}) copy-start(s32[4]{0:T(128)} %param.13) | copy-start | bytes 52
  7.2 16.1 %copy-start.3 = (s32[2,40]{1,0:T(2,128)S(1)}, s32[2,40]{1,0:T(2,128)}, u32[]{:S(2)}) copy-start(s32[2,40]{1,0:T(2,128)} %param.15) | copy-start | bytes 964
  7.2 16.2 %copy-start.5 = (s32[4]{0:T(128)S(1)}, s32[4]{0:T(128)}, u32[]{:S(2)}) copy-start(s32[4]{0:T(128)} %param.14) | copy-start | bytes 52
  7.2 16.3 %copy-start = (bf16[2,2,256,128]{3,2,1,0:T(8,128)(2,1)S(1)}, bf16[2,2,256,128]{3,2,1,0:T(8,128)(2,1)}, u32[]{:S(2)}) copy-start(bf16[2,2,256,128]{3,2,1,0:T(8,128)(2,1)} %param.8) | copy-start | bytes 786436
  7.2 35.7 %reduce-scatter.2.cloned.1.call-start = ((), (), s32[]{:S(2)}) async-start(), calls=%async_computation.1 | async-start | bytes 204800 | tf_op jit(solution)/shard_map/reduce_scatter | solution.py:70
  17.4 28.6 %copy-start.2 = (bf16[2,40,1024]{2,1,0:T(8,128)(2,1)S(1)}, bf16[2,40,1024]{2,1,0:T(8,128)(2,1)}, u32[]{:S(2)}) copy-start(bf16[2,40,1024]{2,1,0:T(8,128)(2,1)} %param.12) | copy-start | bytes 491524
  22.7 50.9 %all-gather.2.cloned.1.call-start = ((), (), s32[]{:S(2)}) async-start(), calls=%async_computation.2 | async-start | bytes 1310720 | tf_op jit(solution)/shard_map/all_gather | solution.py:108
  43.7 32.8 %copy-start.1 = (bf16[2,40,2,128]{3,1,2,0:T(8,128)(2,1)}, bf16[2,40,2,128]{3,1,2,0:T(8,128)(2,1)S(1)}, u32[]{:S(2)}) copy-start(bf16[2,40,2,128]{3,1,2,0:T(8,128)(2,1)S(1)} %copy.48) | copy-start | bytes 122884
Sparse Core Ops, SparseCore 0:
  22.9 20.0 reduce-scatter.1
  45.7 27.9 all-gather.1
where the time goes:
time: 88.9 us; the launch traced here: 88.6 us
  waiting for transfers between devices  46.4 us (52%)
  between operations  14.3 us (16%)
  blocking collectives  8.34 us (9%)
  other arithmetic  7.61 us (9%)
  local copies, waits for them, and re-layouts  6.28 us (7%)
  matrix products  5.58 us (6%)
    all_gather x1, waiting for transfers between devices, local(): block_kv = lax.all_gather(kv_rot, 'seq', axis=0, tiled=True)  27.2 us
    reduce_scatter x1, waiting for transfers between devices, local(): lax.psum_scatter(product.reshape(slot_count * row_count, 1 * lax.axis_siz...  19.2 us
    psum x1, blocking collectives, local(): squares = lax.psum(jnp.sum(inputs * inputs, -1), ('tp', 'kvh'))  8.34 us
    dot_general x1, local copies, waits for them, and re-layouts, local(): product = jnp.dot(normed, kv_weight, preferred_element_type=jnp.float32)  2.89 us
    dot_general x1, matrix products, absorb(): jnp.dot(weight.astype(jnp.bfloat16), value_rows, preferred_element_type=j...  2.27 us
    reduce_sum x1, other arithmetic, absorb(): new_sum = jnp.sum(weight, 1)  2.04 us
  transfers between devices with their start and end apart: 2, of which 2 were waited for; matrix products, arithmetic and copies ran while one was open for 2% of the time, Pallas kernels for 0%

commit v1 on v0

v1 whole, which is shorter than its diff:
```python
import functools
import math

import jax
import jax.numpy as jnp
import numpy as np
from jax import lax
from jax.experimental import pallas as pl
from jax.experimental.pallas import tpu as pltpu
from jax.sharding import PartitionSpec as P

THETA = 500000.0
EPS = 1e-05
FAR = -1e30
FEATURES = ("tp", "kvh")
VMEM = pltpu.MemorySpace.VMEM
SMEM = pltpu.MemorySpace.SMEM


def round_up(value, step):
    return -(-value // step) * step


def rope_tables(positions, width):
    inverse = THETA ** (-2.0 * np.arange(width // 2) / width)
    angle = np.asarray(positions, np.float64)[:, None] * np.concatenate([inverse, inverse])[None]
    return np.cos(angle).astype(np.float32), np.sin(angle).astype(np.float32)


def turn(values, cosine, sine):
    return values * cosine + pltpu.roll(values, values.shape[-1] // 2, 1) * sine


def project_body(me_ref, hidden_ref, gain_ref, weight_ref, *refs):
    del me_ref
    pieces, scaled, tail = refs[:-2], refs[-2], refs[-1]
    step = pl.program_id(0)
    count = scaled.shape[0]
    spare = tail.shape[0]

    @pl.when(step == 0)
    def _():
        hidden = hidden_ref[...].astype(jnp.float32).reshape(count, -1)
        scaled[...] = (hidden * gain_ref[...].astype(jnp.float32)).astype(jnp.bfloat16)
        square = hidden * hidden
        fill = jnp.zeros((round_up(count, 128) - count, square.shape[1]), jnp.float32)
        square = jnp.concatenate([square, fill], 0)
        high = square.astype(jnp.bfloat16)
        low = (square - high.astype(jnp.float32)).astype(jnp.bfloat16)
        ones = jnp.ones((spare, square.shape[1]), jnp.bfloat16)
        along = (((1,), (1,)), ((), ()))
        total = lax.dot_general(ones, high, along, preferred_element_type=jnp.float32)
        total += lax.dot_general(ones, low, along, preferred_element_type=jnp.float32)
        coarse = total.astype(jnp.bfloat16).astype(jnp.float32)
        row = lax.broadcasted_iota(jnp.int32, total.shape, 0)
        both = jnp.where(row == 0, coarse, jnp.where(row == 1, total - coarse, 0.0))
        rest = jnp.zeros((spare, tail.shape[1] - total.shape[1]), jnp.float32)
        tail[...] = jnp.concatenate([both, rest], 1)

    product = jnp.dot(scaled[...], weight_ref[...], preferred_element_type=jnp.float32)
    product = jnp.concatenate([product, tail[...]], 0).astype(jnp.bfloat16)
    for at, piece in enumerate(pieces):

        @pl.when(step == at)
        def _(piece=piece):
            piece[...] = product


def project(me, hidden_rows, norm_gain, kv_weight, parts):
    slots, rows, features = hidden_rows.shape
    count = slots * rows
    columns = kv_weight.shape[1] // parts
    shape = (count + 16, columns)
    return pl.pallas_call(
        project_body,
        out_shape=[jax.ShapeDtypeStruct(shape, jnp.bfloat16)] * parts,
        grid_spec=pltpu.PrefetchScalarGridSpec(
            num_scalar_prefetch=1,
            grid=(parts,),
            in_specs=[
                pl.BlockSpec((slots, rows, features), lambda k, me: (0, 0, 0)),
                pl.BlockSpec((1, features), lambda k, me: (0, 0)),
                pl.BlockSpec((features, columns), lambda k, me: (0, me[0] ^ k)),
            ],
            out_specs=[pl.BlockSpec(shape, lambda k, me: (0, 0))] * parts,
            scratch_shapes=[
                pltpu.VMEM((count, features), jnp.bfloat16),
                pltpu.VMEM((16, columns), jnp.float32),
            ],
        ),
        cost_estimate=pl.CostEstimate(flops=1000, bytes_accessed=1000, transcendentals=0),
        compiler_params=pltpu.CompilerParams(vmem_limit_bytes=48 << 20),
        name="project",
    )(me, hidden_rows, norm_gain.reshape(1, features), kv_weight)


def finish_body(features, marks_ref, *refs):
    pieces, (fresh_ref, payload_ref) = refs[:-2], refs[-2:]
    slots, _, rows, width = fresh_ref.shape
    count = slots * rows
    total = pieces[0][...].astype(jnp.float32)
    for piece in pieces[1:]:
        total += piece[...].astype(jnp.float32)
    lanes = round_up(count, 128)
    squares = total[count : count + 1, :lanes] + total[count + 1 : count + 2, :lanes]
    inverse = lax.rsqrt(squares / features + EPS)
    inverse = jnp.transpose(jnp.broadcast_to(inverse, (lanes, lanes)))[:count, :width]
    for half in range(2):
        values = total[:count, half * width : (half + 1) * width] * inverse
        for slot in range(slots):
            mine = values[slot * rows : (slot + 1) * rows]
            fresh_ref[slot, half] = mine.astype(jnp.bfloat16)
            marked = jnp.concatenate([mine, marks_ref[slot]], 0)
            payload_ref[slot, half] = marked.astype(jnp.bfloat16)


def finish(pieces, marks, slots, rows, width, features):
    return pl.pallas_call(
        functools.partial(finish_body, features),
        out_shape=[
            jax.ShapeDtypeStruct((slots, 2, rows, width), jnp.bfloat16),
            jax.ShapeDtypeStruct((slots, 2, rows + marks.shape[1], width), jnp.bfloat16),
        ],
        cost_estimate=pl.CostEstimate(flops=1000, bytes_accessed=1000, transcendentals=0),
        name="finish",
    )(marks, *pieces)


def attend_body(sizes, locate, slot_ref, length_ref, place_ref, seq_ref, *refs):
    cached_count, fresh_count, rows, span, scale = sizes
    cached, refs = refs[:cached_count], refs[cached_count:]
    fresh, refs = refs[:fresh_count], refs[fresh_count:]
    (query_ref, query_at_ref, query_cos_ref, query_sin_ref, cos_ref, sin_ref, base_cos_ref) = refs[:7]
    base_sin_ref, out_ref = refs[7:9]
    cached_buf, fresh_buf, turned, limit, top, mass, total, sems = refs[9:]
    slots, _, columns = out_ref.shape
    width = cached_buf.shape[-1]
    group = columns // width
    stretches = slot_ref.shape[0]
    factor = scale * math.log2(math.e)
    last = functools.reduce(jnp.maximum, [place_ref[s] for s in range(slots)])

    def copies(position, act):
        slot = slot_ref[position]
        for which, refs, buf in ((0, cached, cached_buf), (1, fresh, fresh_buf)):
            for wanted, piece, index in locate(slot, seq_ref[0], slots, which):

                @pl.when(wanted)
                def _(piece=piece, index=index, refs=refs, buf=buf, which=which):
                    act(
                        pltpu.make_async_copy(
                            refs[piece].at[index], buf.at[position], sems.at[position, which]
                        )
                    )

    def start(position, carry):
        copies(position, lambda copy: copy.start())
        return carry

    lax.fori_loop(0, last + 1, start, 0)

    for slot in range(slots):

        @pl.when(place_ref[slot] >= 0)
        def _(slot=slot):
            cosine, sine = query_cos_ref[slot], query_sin_ref[slot]
            for head in range(group):
                values = query_ref[slot, :, head * width : (head + 1) * width].astype(jnp.float32)
                turned[slot, head * rows : (head + 1) * rows] = turn(values, cosine, sine)
                limit[slot, head * rows : (head + 1) * rows] = query_at_ref[slot]

        @pl.when(place_ref[slot] < 0)
        def _(slot=slot):
            out_ref[slot] = jnp.zeros_like(out_ref[slot])

    flip = jnp.where(lax.broadcasted_iota(jnp.int32, (1, width), 1) < width // 2, -1.0, 1.0)

    def stretch(position, carry):
        copies(position, lambda copy: copy.wait())
        marks = fresh_buf[position, 0, rows - rows % 16 :].astype(jnp.float32)[rows % 16 : rows % 16 + 1]
        token = lax.broadcasted_iota(jnp.int32, (span, width), 0).astype(jnp.float32)
        chosen = jnp.where(token == marks, 1.0, 0.0).astype(jnp.bfloat16)[:, : fresh_buf.shape[2]]
        source = jnp.concatenate(
            [fresh_buf[position, 0], fresh_buf[position, 1], jnp.ones_like(fresh_buf[position, 0])], 1
        )
        placed = jnp.dot(chosen, source, preferred_element_type=jnp.float32)
        replaced = placed[:, 2 * width :] > 0.5
        keys = jnp.where(replaced, placed[:, :width], cached_buf[position, 0].astype(jnp.float32))
        values = jnp.where(
            replaced, placed[:, width : 2 * width], cached_buf[position, 1].astype(jnp.float32)
        ).astype(jnp.bfloat16)
        base_cos, base_sin = base_cos_ref[pl.ds(position, 1)], base_sin_ref[pl.ds(position, 1)]
        cosine = cos_ref[...] * base_cos - sin_ref[...] * base_sin
        sine = (sin_ref[...] * base_cos + cos_ref[...] * base_sin) * flip
        keys = turn(keys, cosine, sine).astype(jnp.bfloat16)
        length = length_ref[position]
        index = lax.broadcasted_iota(jnp.int32, (1, span), 1)

        for slot in range(slots):

            @pl.when(place_ref[slot] >= position)
            def _(slot=slot):
                scores = lax.dot_general(
                    turned[slot].astype(jnp.bfloat16),
                    keys,
                    (((1,), (1,)), ((), ())),
                    preferred_element_type=jnp.float32,
                )
                bound = jnp.minimum(limit[slot] - position * span, length - 1)
                bound = jnp.concatenate([bound] * (span // width), 1)
                scores = jnp.where(index <= bound, scores, FAR)
                here = jnp.max(scores, 1, keepdims=True)

                @pl.when(position == 0)
                def _():
                    weight = jnp.exp2((scores - here) * factor)
                    top[slot] = jnp.broadcast_to(here, top.shape[1:])
                    mass[slot] = jnp.broadcast_to(jnp.sum(weight, 1, keepdims=True), mass.shape[1:])
                    total[slot] = jnp.dot(
                        weight.astype(jnp.bfloat16), values, preferred_element_type=jnp.float32
                    )

                @pl.when(position > 0)
                def _():
                    before = top[slot]
                    after = jnp.maximum(before, here)
                    fade = jnp.exp2((before - after) * factor)
                    weight = jnp.exp2((scores - after[:, :1]) * factor)
                    top[slot] = after
                    mass[slot] = mass[slot] * fade + jnp.sum(weight, 1, keepdims=True)
                    total[slot] = total[slot] * fade + jnp.dot(
                        weight.astype(jnp.bfloat16), values, preferred_element_type=jnp.float32
                    )

        return carry

    lax.fori_loop(0, last + 1, stretch, 0)

    for slot in range(slots):

        @pl.when(place_ref[slot] >= 0)
        def _(slot=slot):
            result = total[slot] / mass[slot]
            for head in range(group):
                out_ref[slot, :, head * width : (head + 1) * width] = result[
                    head * rows : (head + 1) * rows
                ].astype(jnp.bfloat16)


def attend(locate, cached, fresh, tables, queries, stretch_slot, stretch_lengths, my_pos, seq):
    slots, rows, columns = queries.shape
    span, width = cached[0].shape[-2:]
    lines = rows * (columns // width)
    stretches = stretch_slot.shape[0]
    padded = fresh[0].shape[-2]
    sizes = (len(cached), len(fresh), rows, span, width ** (-0.5))
    small = [pl.BlockSpec(memory_space=SMEM)] * 4
    far = [pl.BlockSpec(memory_space=pl.ANY)] * (len(cached) + len(fresh))
    near = [pl.BlockSpec(memory_space=VMEM)] * (1 + len(tables))
    return pl.pallas_call(
        functools.partial(attend_body, sizes, locate),
        out_shape=jax.ShapeDtypeStruct(queries.shape, jnp.bfloat16),
        in_specs=small + far + near,
        out_specs=pl.BlockSpec(memory_space=VMEM),
        scratch_shapes=[
            pltpu.VMEM((stretches, 2, span, width), jnp.bfloat16),
            pltpu.VMEM((stretches, 2, padded, width), jnp.bfloat16),
            pltpu.VMEM((slots, lines, width), jnp.float32),
            pltpu.VMEM((slots, lines, width), jnp.int32),
            pltpu.VMEM((slots, lines, width), jnp.float32),
            pltpu.VMEM((slots, lines, width), jnp.float32),
            pltpu.VMEM((slots, lines, width), jnp.float32),
            pltpu.SemaphoreType.DMA((stretches, 2)),
        ],
        cost_estimate=pl.CostEstimate(flops=1000, bytes_accessed=1000, transcendentals=0),
        compiler_params=pltpu.CompilerParams(vmem_limit_bytes=48 << 20),
        name="attend",
    )(stretch_slot, stretch_lengths, my_pos, seq, *cached, *fresh, queries, *tables)


def locate_gathered(slot, seq, slots, which):
    return [(slot >= 0, 0, slot)]


def locate_exchanged(slot, seq, slots, which):
    away = (slot // slots) ^ seq
    index = slot % slots
    if which == 1:
        return [(away == k, k, index) for k in range(4)]
    return [
        (away == 0, 0, index),
        (away == 1, 1, index),
        ((away == 2) & (index == 0), 2, 0),
        ((away == 3) & (index == 1), 3, 0),
        ((away == 2) & (index == 1), 4, 0),
        ((away == 3) & (index == 0), 5, 0),
    ]


def local(
    pool_kv, hidden_rows, norm_gain, kv_weight, queries, stretch_slot, stretch_lengths, recompute_rows
):
    slots, _, span, width = pool_kv.shape
    rows = recompute_rows.shape[1]
    stretches = stretch_slot.shape[0]
    seq_count = lax.axis_size("seq")
    seq = lax.axis_index("seq")
    parts = lax.axis_size(FEATURES)
    me = lax.axis_index(FEATURES)
    features = hidden_rows.shape[2] * parts
    exchanged = seq_count == 4 and slots == 2

    def along_seq(value, distance):
        return lax.ppermute(value, "seq", [(z, z ^ distance) for z in range(seq_count)])

    if exchanged:
        across = along_seq(pool_kv[0:1], 2)
        astray = along_seq(pool_kv[1:2], 3)
        beside = along_seq(pool_kv, 1)

    pieces = project(me.reshape(1).astype(jnp.int32), hidden_rows, norm_gain, kv_weight, parts)
    sums = [pieces[0]]
    for distance in range(parts - 1, 0, -1):
        sums.append(
            lax.ppermute(pieces[distance], FEATURES, [(i, i ^ distance) for i in range(parts)])
        )
    marks = jnp.pad(recompute_rows.astype(jnp.float32), ((0, 0), (0, width - rows)), constant_values=-1.0)
    marks = jnp.broadcast_to(marks[:, None], (slots, 8, width))
    fresh_kv, payload = finish(sums, marks, slots, rows, width, features)

    mine = seq * slots + jnp.arange(slots, dtype=jnp.int32)
    hits = stretch_slot[:, None] == mine[None]
    order = jnp.arange(stretches, dtype=jnp.int32)[:, None]
    my_pos = jnp.max(jnp.where(hits, order, -1), 0)
    query_at = my_pos[:, None] * span + recompute_rows
    inverse = THETA ** (-2.0 * np.arange(width // 2) / width)
    inverse = np.concatenate([inverse, inverse]).astype(np.float32)
    angle = query_at.astype(jnp.float32)[..., None] * inverse
    flip = np.where(np.arange(width) < width // 2, -1.0, 1.0).astype(np.float32)
    tables = (
        jnp.broadcast_to(query_at[..., None], (slots, rows, width)),
        jnp.cos(angle),
        jnp.sin(angle) * flip,
        *rope_tables(np.arange(span), width),
        *rope_tables(np.arange(stretches) * span, width),
    )

    if exchanged:
        cached = [pool_kv, beside, across, astray, along_seq(astray, 1), along_seq(across, 1)]
        fresh = [payload, along_seq(payload, 1), along_seq(payload, 2), along_seq(payload, 3)]
        locate = locate_exchanged
    else:
        cached = [lax.all_gather(pool_kv, "seq", axis=0, tiled=True)]
        fresh = [lax.all_gather(payload, "seq", axis=0, tiled=True)]
        locate = locate_gathered
    attended = attend(
        locate, cached, fresh, tables, queries, stretch_slot, stretch_lengths, my_pos, seq.reshape(1)
    )
    return fresh_kv, attended


def solution(mesh):
    in_specs = (
        P(("groups", "seq"), None, None, FEATURES),
        P(("groups", "seq"), None, FEATURES),
        P(FEATURES),
        P(FEATURES, None),
        P(("groups", "seq"), None, FEATURES),
        P("groups"),
        P("groups"),
        P(("groups", "seq"), None),
    )
    out_specs = (
        P(("groups", "seq"), None, None, FEATURES),
        P(("groups", "seq"), None, FEATURES),
    )
    return jax.shard_map(local, mesh=mesh, in_specs=in_specs, out_specs=out_specs, check_vma=False)
```

time: 88.9 us -> 42.8 us (0.48)
  the two profiles are of different devices: /device:TPU:0 before, /device:TPU:6 now
where the time goes in v1:
time: 42.8 us; the launch traced here: 42.4 us
  starting transfers between devices  18.4 us (43%)
  Pallas kernels  9 us (21%)
  waiting for transfers between devices  8.89 us (21%)
  local copies, waits for them, and re-layouts  4.77 us (11%)
  between operations  0.86 us (2%)
  other arithmetic  0.49 us (1%)
    ppermute x8, starting transfers between devices, along_seq(): lax.ppermute(value, 'seq', [(z, z ^ distance) for z in range(seq_count)])  16.4 us
    ppermute x8, waiting for transfers between devices, along_seq(): lax.ppermute(value, 'seq', [(z, z ^ distance) for z in range(seq_count)])  8.88 us
    pallas_call x1, Pallas kernels, attend(): pl.pallas_call(functools.partial(attend_body, sizes, locate), out_shape=j...  5.84 us
    unnamed x36, local copies, waits for them, and re-layouts  3.37 us
    ppermute x3, starting transfers between devices, local(): lax.ppermute(pieces[distance], FEATURES, [(i, i ^ distance) for i in rang...  1.92 us
    pallas_call x1, Pallas kernels, finish(): pl.pallas_call(functools.partial(finish_body, features), out_shape=[jax.S...  1.62 us
    pallas_call x1, Pallas kernels, project(): pl.pallas_call(project_body, out_shape=[jax.ShapeDtypeStruct(shape, jnp.b...  1.54 us
  transfers between devices with their start and end apart: 11, of which 4 were waited for; matrix products, arithmetic and copies ran while one was open for 3% of the time, Pallas kernels for 4%

profile of v1, /device:TPU:6, one launch (start us, length us, event | category | flops | bytes accessed | tf_op | source)
XLA Modules:
  0.0 42.4 jit_solution(16417052500571868421)
XLA Ops:
  0.7 0.7 %reshape.28.gain_ref = bf16[1,1024]{1,0:T(2,128)(2,1)S(1)} reshape(bf16[1024]{0:T(1024)(128)(2,1)} %param.16) | data formatting | bytes 4096 | tf_op jit(solution)/shard_map/reshape | solution.py:94
  1.4 1.6 %copy-done = bf16[1024,1024]{1,0:T(8,128)(2,1)S(1)} copy-done((bf16[1024,1024]{1,0:T(8,128)(2,1)S(1)}, bf16[1024,1024]{1,0:T(8,128)(2,1)}, u32[]{:S(2)}) %copy-start) | copy-done | bytes 2097176
  3.0 0.9 %copy-done.2 = bf16[2,40,1024]{2,1,0:T(8,128)(2,1)S(1)} copy-done((bf16[2,40,1024]{2,1,0:T(8,128)(2,1)S(1)}, bf16[2,40,1024]{2,1,0:T(8,128)(2,1)}, u32[]{:S(2)}) %copy-start.2) | copy-done | bytes 163864
  3.9 1.5 %project.1 = (bf16[96,256]{1,0:T(8,128)(2,1)S(1)}, bf16[96,256]{1,0:T(8,128)(2,1)S(1)}, bf16[96,256]{1,0:T(8,128)(2,1)S(1)}, bf16[96,256]{1,0:T(8,128)(2,1)S(1)}) custom-call(s32[1]{0:T(128)} %bitcast.me_ref, bf16[2,40,1024]{2,1,0:T(8,128)(2,1)S(1)} %copy-done.2, bf16[1,1024]{1,0:T(2,128)(2,1)S(1)} %reshape.28.gain_ref, bf16[1024,1024]{1,0:T(8,128)(2,1)S(1)} %copy-done), custom_call_target="tpu_custom_call" | custom-call | flops 1000 | bytes 1000 | tf_op jit(solution)/shard_map/project/pallas_call | solution.py:74
  5.6 1.5 %collective-permute-start.1 = (bf16[96,256]{1,0:T(8,128)(2,1)S(1)}, bf16[96,256]{1,0:T(8,128)(2,1)S(1)}, u32[]{:S(2)}, u32[]{:S(2)}) collective-permute-start(bf16[96,256]{1,0:T(8,128)(2,1)S(1)} %get-tuple-element.10), channel_id=1, source_target_pairs={{0,2},{1,3},{2,0},{3,1},{4,6},{5,7},{6,4},{7,5},{8,10},{9,11},{10,... | collective-permute-start | bytes 147464 | tf_op jit(solution)/shard_map/ppermute | solution.py:325
  7.0 0.4 collective-permute-start.2
  7.4 3.7 %collective-permute-start.5 = (bf16[1,2,256,128]{3,2,1,0:T(8,128)(2,1)S(1)}, bf16[1,2,256,128]{3,2,1,0:T(8,128)(2,1)S(1)}, u32[]{:S(2)}, u32[]{:S(2)}) collective-permute-start(bf16[1,2,256,128]{3,2,1,0:T(8,128)(2,1)S(1)} %get-tuple-element.16), channel_id=1, source_target_pairs={{0,12},{4,8},{8,4},{12,0},{1,13},{5,9},{9,5},{13,1},{2,14},{6,10},... | collective-permute-start | bytes 393224 | tf_op jit(solution)/shard_map/ppermute | solution.py:314
  11.1 0.2 fusion.1.place_ref
  11.3 0.1 fusion.2
  11.5 0.6 %broadcast_in_dim.16.marks_ref = f32[2,8,128]{2,1,0:T(8,128)} broadcast(f32[2,128]{1,0:T(2,128)S(1)} %pad.4), dimensions={0,2} | broadcast | bytes 9216 | tf_op jit(solution)/shard_map/broadcast_in_dim | solution.py:328
  12.1 1.6 %finish.1 = (bf16[2,2,40,128]{3,2,1,0:T(8,128)(2,1)}, bf16[2,2,48,128]{3,2,1,0:T(8,128)(2,1)}) custom-call(f32[2,8,128]{2,1,0:T(8,128)} %broadcast_in_dim.16.marks_ref, bf16[96,256]{1,0:T(8,128)(2,1)} %copy-done.6, bf16[96,256]{1,0:T(8,128)(2,1)} %copy-done.12, bf16[96,256]{1,0:T(8,128)(2,1)} %copy-done.13, bf16[96,256]{1,0:T(8,128)(2,1)} %copy-done.14), custom_call_target="tpu_custom_call" | custom-call | flops 1000 | bytes 1000 | tf_op jit(solution)/shard_map/finish/pallas_call | solution.py:118
  13.7 2.8 %collective-permute-start.10 = (bf16[2,2,48,128]{3,2,1,0:T(8,128)(2,1)}, bf16[2,2,48,128]{3,2,1,0:T(8,128)(2,1)S(1)}, u32[]{:S(2)}, u32[]{:S(2)}) collective-permute-start(bf16[2,2,48,128]{3,2,1,0:T(8,128)(2,1)} %get-tuple-element.13.refs_6_), channel_id=1, source_target_pairs={{0,12},{4,8},{8,4},{12,0},{1,13},{5,9},{9,5},{13,1},{2,14},{6,10},... | collective-permute-start | bytes 147464 | tf_op jit(solution)/shard_map/ppermute | solution.py:314
  16.5 0.7 %collective-permute-start.3 = (bf16[2,2,256,128]{3,2,1,0:T(8,128)(2,1)S(1)}, bf16[2,2,256,128]{3,2,1,0:T(8,128)(2,1)S(1)}, u32[]{:S(2)}, u32[]{:S(2)}) collective-permute-start(bf16[2,2,256,128]{3,2,1,0:T(8,128)(2,1)S(1)} %copy-done.1), channel_id=1, source_target_pairs={{0,4},{4,0},{8,12},{12,8},{1,5},{5,1},{9,13},{13,9},{2,6},{6,2},{1... | collective-permute-start | bytes 786440 | tf_op jit(solution)/shard_map/ppermute | solution.py:314
  17.2 0.9 %collective-permute-start.9 = (bf16[2,2,48,128]{3,2,1,0:T(8,128)(2,1)}, bf16[2,2,48,128]{3,2,1,0:T(8,128)(2,1)S(1)}, u32[]{:S(2)}, u32[]{:S(2)}) collective-permute-start(bf16[2,2,48,128]{3,2,1,0:T(8,128)(2,1)} %get-tuple-element.13.refs_6_), channel_id=1, source_target_pairs={{0,8},{4,12},{8,0},{12,4},{1,9},{5,13},{9,1},{13,5},{2,10},{6,14},... | collective-permute-start | bytes 147464 | tf_op jit(solution)/shard_map/ppermute | solution.py:314
  18.1 2.3 %collective-permute-done.10.refs_9_ = bf16[2,2,48,128]{3,2,1,0:T(8,128)(2,1)S(1)} collective-permute-done((bf16[2,2,48,128]{3,2,1,0:T(8,128)(2,1)}, bf16[2,2,48,128]{3,2,1,0:T(8,128)(2,1)S(1)}, u32[]{:S(2)}, u32[]{:S(2)}) %collective-permute-start.10) | collective-permute-done | bytes 49184 | tf_op jit(solution)/shard_map/ppermute | solution.py:314
  20.4 6.4 %collective-permute-start.8 = (bf16[2,2,48,128]{3,2,1,0:T(8,128)(2,1)}, bf16[2,2,48,128]{3,2,1,0:T(8,128)(2,1)S(1)}, u32[]{:S(2)}, u32[]{:S(2)}) collective-permute-start(bf16[2,2,48,128]{3,2,1,0:T(8,128)(2,1)} %get-tuple-element.13.refs_6_), channel_id=1, source_target_pairs={{0,4},{4,0},{8,12},{12,8},{1,5},{5,1},{9,13},{13,9},{2,6},{6,2},{1... | collective-permute-start | bytes 147464 | tf_op jit(solution)/shard_map/ppermute | solution.py:314
  26.8 2.0 %collective-permute-start.7 = (bf16[1,2,256,128]{3,2,1,0:T(8,128)(2,1)S(1)}, bf16[1,2,256,128]{3,2,1,0:T(8,128)(2,1)S(1)}, u32[]{:S(2)}, u32[]{:S(2)}) collective-permute-start(bf16[1,2,256,128]{3,2,1,0:T(8,128)(2,1)S(1)} %collective-permute-done.4.refs_2_), channel_id=1, source_target_pairs={{0,4},{4,0},{8,12},{12,8},{1,5},{5,1},{9,13},{13,9},{2,6},{6,2},{1... | collective-permute-start | bytes 393224 | tf_op jit(solution)/shard_map/ppermute | solution.py:314
  28.8 0.2 fusion
  29.0 1.6 %collective-permute-done.8.refs_7_ = bf16[2,2,48,128]{3,2,1,0:T(8,128)(2,1)S(1)} collective-permute-done((bf16[2,2,48,128]{3,2,1,0:T(8,128)(2,1)}, bf16[2,2,48,128]{3,2,1,0:T(8,128)(2,1)S(1)}, u32[]{:S(2)}, u32[]{:S(2)}) %collective-permute-start.8) | collective-permute-done | bytes 49184 | tf_op jit(solution)/shard_map/ppermute | solution.py:314
  30.6 2.8 %collective-permute-done.6.refs_4_ = bf16[1,2,256,128]{3,2,1,0:T(8,128)(2,1)S(1)} collective-permute-done((bf16[1,2,256,128]{3,2,1,0:T(8,128)(2,1)S(1)}, bf16[1,2,256,128]{3,2,1,0:T(8,128)(2,1)S(1)}, u32[]{:S(2)}, u32[]{:S(2)}) %collective-permute-start.6) | collective-permute-done | bytes 131104 | tf_op jit(solution)/shard_map/ppermute | solution.py:314
  33.4 2.2 %collective-permute-done.7.refs_5_ = bf16[1,2,256,128]{3,2,1,0:T(8,128)(2,1)S(1)} collective-permute-done((bf16[1,2,256,128]{3,2,1,0:T(8,128)(2,1)S(1)}, bf16[1,2,256,128]{3,2,1,0:T(8,128)(2,1)S(1)}, u32[]{:S(2)}, u32[]{:S(2)}) %collective-permute-start.7) | collective-permute-done | bytes 131104 | tf_op jit(solution)/shard_map/ppermute | solution.py:314
  35.6 0.1 broadcast_in_dim.19.refs_11_
  35.8 0.8 %copy-done.7 = bf16[2,2,48,128]{3,2,1,0:T(8,128)(2,1)S(1)} copy-done((bf16[2,2,48,128]{3,2,1,0:T(8,128)(2,1)S(1)}, bf16[2,2,48,128]{3,2,1,0:T(8,128)(2,1)}, u32[]{:S(2)}) %copy-start.7) | copy-done | bytes 49176
  36.5 5.8 %attend.1 = bf16[2,40,1024]{2,1,0:T(8,128)(2,1)} custom-call(s32[4]{0:T(128)S(1)} %copy-done.10, s32[4]{0:T(128)S(1)} %copy-done.11, s32[2]{0:T(128)S(1)} %fusion.1.place_ref, s32[1]{0:T(128)} %bitcast.1.seq_ref, bf16[2,2,256,128]{3,2,1,0:T(8,128)(2,1)S(1)} %copy-done.1, bf16[2,2,256,128]{3,2,1,0:T(8,128)(2,1)S(1)} %collective-permute-done.3.refs_1_, ...), custom_call_target="tpu_custom_call" | custom-call | flops 1000 | bytes 1000 | tf_op jit(solution)/shard_map/attend/pallas_call | solution.py:260
  (47 shorter events, 0.2 us)
Async XLA Ops:
  0.6 28.1 %copy-start.16 = (f32[128]{0:T(128)S(1)}, f32[128]{0:T(128)}, u32[]{:S(2)}) copy-start(f32[128]{0:T(128)} %constant.34.clone) | copy-start | bytes 1540
  0.6 28.1 %copy-start.17 = (f32[128]{0:T(128)S(1)}, f32[128]{0:T(128)}, u32[]{:S(2)}) copy-start(f32[128]{0:T(128)} %constant.33.clone) | copy-start | bytes 1540
  0.7 35.0 %copy-start.8 = (f32[4,128]{1,0:T(4,128)S(1)}, f32[4,128]{1,0:T(4,128)}, u32[]{:S(2)}) copy-start(f32[4,128]{1,0:T(4,128)} %constant.38.clone.refs_17_) | copy-start | bytes 6148
  0.7 35.0 %copy-start.9 = (f32[4,128]{1,0:T(4,128)S(1)}, f32[4,128]{1,0:T(4,128)}, u32[]{:S(2)}) copy-start(f32[4,128]{1,0:T(4,128)} %constant.37.clone.refs_16_) | copy-start | bytes 6148
  0.7 10.4 %copy-start.10 = (s32[4]{0:T(128)S(1)}, s32[4]{0:T(128)}, u32[]{:S(2)}) copy-start(s32[4]{0:T(128)} %slot_ref.1) | copy-start | bytes 52
  0.7 10.6 %copy-start.15 = (s32[2,40]{1,0:T(2,128)S(1)}, s32[2,40]{1,0:T(2,128)}, u32[]{:S(2)}) copy-start(s32[2,40]{1,0:T(2,128)} %param.21) | copy-start | bytes 964
  0.7 35.0 %copy-start.11 = (s32[4]{0:T(128)S(1)}, s32[4]{0:T(128)}, u32[]{:S(2)}) copy-start(s32[4]{0:T(128)} %length_ref.1) | copy-start | bytes 52
  1.4 1.6 %copy-start = (bf16[1024,1024]{1,0:T(8,128)(2,1)S(1)}, bf16[1024,1024]{1,0:T(8,128)(2,1)}, u32[]{:S(2)}) copy-start(bf16[1024,1024]{1,0:T(8,128)(2,1)} %weight_ref.1) | copy-start | bytes 6291460
  3.9 3.5 %copy-start.1 = (bf16[2,2,256,128]{3,2,1,0:T(8,128)(2,1)S(1)}, bf16[2,2,256,128]{3,2,1,0:T(8,128)(2,1)}, u32[]{:S(2)}) copy-start(bf16[2,2,256,128]{3,2,1,0:T(8,128)(2,1)} %refs_0_.1) | copy-start | bytes 786436
  3.9 31.8 %copy-start.3 = (bf16[2,40,1024]{2,1,0:T(8,128)(2,1)S(1)}, bf16[2,40,1024]{2,1,0:T(8,128)(2,1)}, u32[]{:S(2)}) copy-start(bf16[2,40,1024]{2,1,0:T(8,128)(2,1)} %refs_10_.1) | copy-start | bytes 491524
  3.9 31.8 %copy-start.4 = (f32[256,128]{1,0:T(8,128)S(1)}, f32[256,128]{1,0:T(8,128)}, u32[]{:S(2)}) copy-start(f32[256,128]{1,0:T(8,128)} %constant.36.clone.refs_15_) | copy-start | bytes 393220
  3.9 31.8 %copy-start.5 = (f32[256,128]{1,0:T(8,128)S(1)}, f32[256,128]{1,0:T(8,128)}, u32[]{:S(2)}) copy-start(f32[256,128]{1,0:T(8,128)} %constant.35.clone.refs_14_) | copy-start | bytes 393220
  5.5 5.6 %copy-start.6 = (bf16[96,256]{1,0:T(8,128)(2,1)}, bf16[96,256]{1,0:T(8,128)(2,1)S(1)}, u32[]{:S(2)}) copy-start(bf16[96,256]{1,0:T(8,128)(2,1)S(1)} %get-tuple-element.8.refs_0_) | copy-start | bytes 147460
  5.5 5.9 %collective-permute-start = (bf16[96,256]{1,0:T(8,128)(2,1)S(1)}, bf16[96,256]{1,0:T(8,128)(2,1)S(1)}, u32[]{:S(2)}, u32[]{:S(2)}) collective-permute-start(bf16[96,256]{1,0:T(8,128)(2,1)S(1)} %get-tuple-element.9), channel_id=1, source_target_pairs={{0,3},{1,2},{2,1},{3,0},{4,7},{5,6},{6,5},{7,4},{8,11},{9,10},{10,... | collective-permute-start | bytes 147464 | tf_op jit(solution)/shard_map/ppermute | solution.py:325
  5.6 5.9 %collective-permute-start.1 = (bf16[96,256]{1,0:T(8,128)(2,1)S(1)}, bf16[96,256]{1,0:T(8,128)(2,1)S(1)}, u32[]{:S(2)}, u32[]{:S(2)}) collective-permute-start(bf16[96,256]{1,0:T(8,128)(2,1)S(1)} %get-tuple-element.10), channel_id=1, source_target_pairs={{0,2},{1,3},{2,0},{3,1},{4,6},{5,7},{6,4},{7,5},{8,10},{9,11},{10,... | collective-permute-start | bytes 147464 | tf_op jit(solution)/shard_map/ppermute | solution.py:325
  7.0 4.4 %collective-permute-start.2 = (bf16[96,256]{1,0:T(8,128)(2,1)S(1)}, bf16[96,256]{1,0:T(8,128)(2,1)S(1)}, u32[]{:S(2)}, u32[]{:S(2)}) collective-permute-start(bf16[96,256]{1,0:T(8,128)(2,1)S(1)} %get-tuple-element.11), channel_id=1, source_target_pairs={{0,1},{1,0},{2,3},{3,2},{4,5},{5,4},{6,7},{7,6},{8,9},{9,8},{10,11... | collective-permute-start | bytes 147464 | tf_op jit(solution)/shard_map/ppermute | solution.py:325
  7.4 19.3 %collective-permute-start.5 = (bf16[1,2,256,128]{3,2,1,0:T(8,128)(2,1)S(1)}, bf16[1,2,256,128]{3,2,1,0:T(8,128)(2,1)S(1)}, u32[]{:S(2)}, u32[]{:S(2)}) collective-permute-start(bf16[1,2,256,128]{3,2,1,0:T(8,128)(2,1)S(1)} %get-tuple-element.16), channel_id=1, source_target_pairs={{0,12},{4,8},{8,4},{12,0},{1,13},{5,9},{9,5},{13,1},{2,14},{6,10},... | collective-permute-start | bytes 393224 | tf_op jit(solution)/shard_map/ppermute | solution.py:314
  11.1 15.6 %collective-permute-start.4 = (bf16[1,2,256,128]{3,2,1,0:T(8,128)(2,1)S(1)}, bf16[1,2,256,128]{3,2,1,0:T(8,128)(2,1)S(1)}, u32[]{:S(2)}, u32[]{:S(2)}) collective-permute-start(bf16[1,2,256,128]{3,2,1,0:T(8,128)(2,1)S(1)} %get-tuple-element.17), channel_id=1, source_target_pairs={{0,8},{4,12},{8,0},{12,4},{1,9},{5,13},{9,1},{13,5},{2,10},{6,14},... | collective-permute-start | bytes 393224 | tf_op jit(solution)/shard_map/ppermute | solution.py:314
  13.7 6.6 %collective-permute-start.10 = (bf16[2,2,48,128]{3,2,1,0:T(8,128)(2,1)}, bf16[2,2,48,128]{3,2,1,0:T(8,128)(2,1)S(1)}, u32[]{:S(2)}, u32[]{:S(2)}) collective-permute-start(bf16[2,2,48,128]{3,2,1,0:T(8,128)(2,1)} %get-tuple-element.13.refs_6_), channel_id=1, source_target_pairs={{0,12},{4,8},{8,4},{12,0},{1,13},{5,9},{9,5},{13,1},{2,14},{6,10},... | collective-permute-start | bytes 147464 | tf_op jit(solution)/shard_map/ppermute | solution.py:314
  16.5 19.1 %collective-permute-start.3 = (bf16[2,2,256,128]{3,2,1,0:T(8,128)(2,1)S(1)}, bf16[2,2,256,128]{3,2,1,0:T(8,128)(2,1)S(1)}, u32[]{:S(2)}, u32[]{:S(2)}) collective-permute-start(bf16[2,2,256,128]{3,2,1,0:T(8,128)(2,1)S(1)} %copy-done.1), channel_id=1, source_target_pairs={{0,4},{4,0},{8,12},{12,8},{1,5},{5,1},{9,13},{13,9},{2,6},{6,2},{1... | collective-permute-start | bytes 786440 | tf_op jit(solution)/shard_map/ppermute | solution.py:314
  17.2 11.8 %collective-permute-start.9 = (bf16[2,2,48,128]{3,2,1,0:T(8,128)(2,1)}, bf16[2,2,48,128]{3,2,1,0:T(8,128)(2,1)S(1)}, u32[]{:S(2)}, u32[]{:S(2)}) collective-permute-start(bf16[2,2,48,128]{3,2,1,0:T(8,128)(2,1)} %get-tuple-element.13.refs_6_), channel_id=1, source_target_pairs={{0,8},{4,12},{8,0},{12,4},{1,9},{5,13},{9,1},{13,5},{2,10},{6,14},... | collective-permute-start | bytes 147464 | tf_op jit(solution)/shard_map/ppermute | solution.py:314
  20.4 10.2 %collective-permute-start.8 = (bf16[2,2,48,128]{3,2,1,0:T(8,128)(2,1)}, bf16[2,2,48,128]{3,2,1,0:T(8,128)(2,1)S(1)}, u32[]{:S(2)}, u32[]{:S(2)}) collective-permute-start(bf16[2,2,48,128]{3,2,1,0:T(8,128)(2,1)} %get-tuple-element.13.refs_6_), channel_id=1, source_target_pairs={{0,4},{4,0},{8,12},{12,8},{1,5},{5,1},{9,13},{13,9},{2,6},{6,2},{1... | collective-permute-start | bytes 147464 | tf_op jit(solution)/shard_map/ppermute | solution.py:314
  26.7 6.7 %collective-permute-start.6 = (bf16[1,2,256,128]{3,2,1,0:T(8,128)(2,1)S(1)}, bf16[1,2,256,128]{3,2,1,0:T(8,128)(2,1)S(1)}, u32[]{:S(2)}, u32[]{:S(2)}) collective-permute-start(bf16[1,2,256,128]{3,2,1,0:T(8,128)(2,1)S(1)} %collective-permute-done.5.refs_3_), channel_id=1, source_target_pairs={{0,4},{4,0},{8,12},{12,8},{1,5},{5,1},{9,13},{13,9},{2,6},{6,2},{1... | collective-permute-start | bytes 393224 | tf_op jit(solution)/shard_map/ppermute | solution.py:314
  26.8 8.9 %collective-permute-start.7 = (bf16[1,2,256,128]{3,2,1,0:T(8,128)(2,1)S(1)}, bf16[1,2,256,128]{3,2,1,0:T(8,128)(2,1)S(1)}, u32[]{:S(2)}, u32[]{:S(2)}) collective-permute-start(bf16[1,2,256,128]{3,2,1,0:T(8,128)(2,1)S(1)} %collective-permute-done.4.refs_2_), channel_id=1, source_target_pairs={{0,4},{4,0},{8,12},{12,8},{1,5},{5,1},{9,13},{13,9},{2,6},{6,2},{1... | collective-permute-start | bytes 393224 | tf_op jit(solution)/shard_map/ppermute | solution.py:314
  (5 other events, 3.7 us)

commit v2 on v1

v2 whole, which is shorter than its diff:
```python
import functools
import math

import jax
import jax.numpy as jnp
import numpy as np
from jax import lax
from jax.experimental import pallas as pl
from jax.experimental.pallas import tpu as pltpu
from jax.sharding import PartitionSpec as P

THETA = 500000.0
EPS = 1e-05
FAR = -1e30
FEATURES = ("tp", "kvh")
VMEM = pltpu.MemorySpace.VMEM
SMEM = pltpu.MemorySpace.SMEM
PROJECT_VMEM = 61 << 20


def round_up(value, step):
    return -(-value // step) * step


def rope_tables(positions, width):
    inverse = THETA ** (-2.0 * np.arange(width // 2) / width)
    angle = np.asarray(positions, np.float64)[:, None] * np.concatenate([inverse, inverse])[None]
    return np.cos(angle).astype(np.float32), np.sin(angle).astype(np.float32)


def turn(values, cosine, sine):
    return values * cosine + pltpu.roll(values, values.shape[-1] // 2, 1) * sine


def project_body(me_ref, hidden_ref, gain_ref, weight_ref, *refs):
    pieces, (held, gain, weights, whole, sems) = refs[:-5], refs[-5:]
    chunks, depth, width = weights.shape
    slots, rows, features = held.shape
    count = slots * rows
    height, columns = pieces[0].shape
    spare = height - count

    def chunk(k):
        part = weight_ref.at[pl.ds(k * depth, depth)]
        return pltpu.make_async_copy(part, weights.at[k], sems.at[2 + k])

    arrive = pltpu.make_async_copy(hidden_ref, held, sems.at[0])
    follow = pltpu.make_async_copy(gain_ref, gain, sems.at[1])
    arrive.start()
    follow.start()
    for k in range(chunks):
        chunk(k).start()
    arrive.wait()
    follow.wait()
    hidden = held[...].astype(jnp.float32).reshape(count, features)
    scaled = (hidden * gain[...].astype(jnp.float32).reshape(1, features)).astype(jnp.bfloat16)
    square = hidden * hidden
    fill = jnp.zeros((round_up(count, 128) - count, features), jnp.float32)
    square = jnp.concatenate([square, fill], 0)
    high = square.astype(jnp.bfloat16)
    low = (square - high.astype(jnp.float32)).astype(jnp.bfloat16)
    ones = jnp.ones((spare, features), jnp.bfloat16)
    along = (((1,), (1,)), ((), ()))
    total = lax.dot_general(ones, high, along, preferred_element_type=jnp.float32)
    total += lax.dot_general(ones, low, along, preferred_element_type=jnp.float32)
    coarse = total.astype(jnp.bfloat16).astype(jnp.float32)
    row = lax.broadcasted_iota(jnp.int32, total.shape, 0)
    both = jnp.where(row == 0, coarse, jnp.where(row == 1, total - coarse, 0.0))
    rest = jnp.zeros((spare, columns - total.shape[1]), jnp.float32)
    tail = jnp.concatenate([both, rest], 1).astype(jnp.bfloat16)
    product = jnp.zeros((count, width), jnp.float32)
    for k in range(chunks):
        chunk(k).wait()
        part = scaled[:, k * depth : (k + 1) * depth]
        product += jnp.dot(part, weights[k], preferred_element_type=jnp.float32)
    whole[...] = product
    for k, piece in enumerate(pieces):
        at = pl.multiple_of((me_ref[0] ^ k) * columns, columns)
        piece[:count] = whole[:, pl.ds(at, columns)].astype(jnp.bfloat16)
        piece[count:] = tail


def project(me, hidden_rows, norm_gain, kv_weight, parts):
    slots, rows, features = hidden_rows.shape
    columns = kv_weight.shape[1] // parts
    chunks = 4
    shape = (slots * rows + 16, columns)
    return pl.pallas_call(
        project_body,
        out_shape=[jax.ShapeDtypeStruct(shape, jnp.bfloat16)] * parts,
        in_specs=[pl.BlockSpec(memory_space=SMEM)] + [pl.BlockSpec(memory_space=pltpu.HBM)] * 3,
        out_specs=[pl.BlockSpec(memory_space=VMEM)] * parts,
        scratch_shapes=[
            pltpu.VMEM(hidden_rows.shape, jnp.bfloat16),
            pltpu.VMEM(norm_gain.shape, jnp.bfloat16),
            pltpu.VMEM((chunks, features // chunks, kv_weight.shape[1]), jnp.bfloat16),
            pltpu.VMEM((slots * rows, kv_weight.shape[1]), jnp.float32),
            pltpu.SemaphoreType.DMA((2 + chunks,)),
        ],
        cost_estimate=pl.CostEstimate(flops=1000, bytes_accessed=1000, transcendentals=0),
        compiler_params=pltpu.CompilerParams(vmem_limit_bytes=PROJECT_VMEM),
        name="project",
    )(me, hidden_rows, norm_gain, kv_weight)


def finish_body(features, marks_ref, *refs):
    pieces, (fresh_ref, payload_ref) = refs[:-2], refs[-2:]
    slots, _, rows, width = fresh_ref.shape
    count = slots * rows
    total = pieces[0][...].astype(jnp.float32)
    for piece in pieces[1:]:
        total += piece[...].astype(jnp.float32)
    lanes = round_up(count, 128)
    squares = total[count : count + 1, :lanes] + total[count + 1 : count + 2, :lanes]
    inverse = lax.rsqrt(squares / features + EPS)
    inverse = jnp.transpose(jnp.broadcast_to(inverse, (lanes, lanes)))[:count, :width]
    for half in range(2):
        values = total[:count, half * width : (half + 1) * width] * inverse
        for slot in range(slots):
            mine = values[slot * rows : (slot + 1) * rows]
            fresh_ref[slot, half] = mine.astype(jnp.bfloat16)
            marks = jnp.broadcast_to(marks_ref[slot : slot + 1], (payload_ref.shape[2] - rows, width))
            marked = jnp.concatenate([mine, marks], 0)
            payload_ref[slot, half] = marked.astype(jnp.bfloat16)


def finish(pieces, marks, slots, rows, width, features):
    return pl.pallas_call(
        functools.partial(finish_body, features),
        out_shape=[
            jax.ShapeDtypeStruct((slots, 2, rows, width), jnp.bfloat16),
            jax.ShapeDtypeStruct((slots, 2, round_up(rows + 1, 16), width), jnp.bfloat16),
        ],
        cost_estimate=pl.CostEstimate(flops=1000, bytes_accessed=1000, transcendentals=0),
        compiler_params=pltpu.CompilerParams(vmem_limit_bytes=8 << 20),
        name="finish",
    )(marks, *pieces)


def tie_body(*refs):
    pass


def tie(value, others):
    return pl.pallas_call(
        tie_body,
        out_shape=jax.ShapeDtypeStruct(value.shape, value.dtype),
        in_specs=[pl.BlockSpec(memory_space=pl.ANY)] * (1 + len(others)),
        out_specs=pl.BlockSpec(memory_space=pl.ANY),
        input_output_aliases={0: 0},
        cost_estimate=pl.CostEstimate(flops=1000, bytes_accessed=1000, transcendentals=0),
        compiler_params=pltpu.CompilerParams(vmem_limit_bytes=1 << 20),
        name="tie",
    )(value, *others)


def ready(cached_buf, fresh_buf, position, rows, tables):
    cos_ref, sin_ref, base_cos_ref, base_sin_ref = tables
    span, width = cached_buf.shape[-2:]
    start = rows - rows % 16
    marks = fresh_buf[position, 0, start:].astype(jnp.float32)[rows - start : rows - start + 1]
    token = lax.broadcasted_iota(jnp.int32, (span, width), 0).astype(jnp.float32)
    chosen = jnp.where(token == marks, 1.0, 0.0).astype(jnp.bfloat16)[:, : fresh_buf.shape[-2]]
    keys, values = fresh_buf[position, 0], fresh_buf[position, 1]
    source = jnp.concatenate([keys, values, jnp.ones_like(keys)], 1)
    placed = jnp.dot(chosen, source, preferred_element_type=jnp.float32)
    replaced = placed[:, 2 * width :] > 0.5
    old_keys, old_values = cached_buf[position, 0], cached_buf[position, 1]
    keys = jnp.where(replaced, placed[:, :width], old_keys.astype(jnp.float32))
    values = jnp.where(replaced, placed[:, width : 2 * width], old_values.astype(jnp.float32))
    base_cos, base_sin = base_cos_ref[pl.ds(position, 1)], base_sin_ref[pl.ds(position, 1)]
    flip = jnp.where(lax.broadcasted_iota(jnp.int32, (1, width), 1) < width // 2, -1.0, 1.0)
    cosine = cos_ref[...] * base_cos - sin_ref[...] * base_sin
    sine = (sin_ref[...] * base_cos + cos_ref[...] * base_sin) * flip
    return turn(keys, cosine, sine).astype(jnp.bfloat16), values.astype(jnp.bfloat16)


def fetch(act, places, cached, fresh, cached_buf, fresh_buf, sems, position):
    for wanted, piece, index in places:

        @pl.when(wanted)
        def _(piece=piece, index=index):
            for which, refs, buf in ((0, cached, cached_buf), (1, fresh, fresh_buf)):
                act(
                    pltpu.make_async_copy(
                        refs[piece].at[index], buf.at[position], sems.at[position, which]
                    )
                )


def score(query, keys):
    along = (((1,), (1,)), ((), ()))
    return lax.dot_general(query, keys, along, preferred_element_type=jnp.float32)


def absorb(first, state, scores, values, factor):
    top, mass, total = state
    before = jnp.where(first, FAR, top[...])
    after = jnp.maximum(before, jnp.max(scores, 1, keepdims=True))
    fade = jnp.where(first, 0.0, jnp.exp2((before - after) * factor))
    weight = jnp.exp2((scores - after[:, :1]) * factor)
    top[...] = after
    mass[...] = jnp.where(first, 0.0, mass[...]) * fade + jnp.sum(weight, 1, keepdims=True)
    total[...] = jnp.where(first, 0.0, total[...]) * fade + jnp.dot(
        weight.astype(jnp.bfloat16), values, preferred_element_type=jnp.float32
    )


def early_body(pieces, locate, rows, factor, slot_ref, length_ref, place_ref, seq_ref, *refs):
    cached, fresh, refs = refs[:pieces], refs[pieces : 2 * pieces], refs[2 * pieces :]
    query_ref, query_at_ref, query_cos_ref, query_sin_ref, *tables = refs[:8]
    turned, top, mass, total, cached_buf, fresh_buf, keys_buf, values_buf, sems = refs[8:]
    slots, _, columns = query_ref.shape
    span, width = cached_buf.shape[-2:]
    group = columns // width
    stretches = slot_ref.shape[0]
    last = functools.reduce(jnp.maximum, [place_ref[s] for s in range(slots)])

    def there(position):
        places = locate(slot_ref[position], seq_ref[0], slots)
        return functools.reduce(jnp.logical_or, [place[0] for place in places])

    def copies(position, act):
        places = locate(slot_ref[position], seq_ref[0], slots)
        fetch(act, places, cached, fresh, cached_buf, fresh_buf, sems, position)

    def start(position, carry):
        copies(position, lambda copy: copy.start())

        @pl.when(jnp.logical_not(there(position)))
        def _():
            cached_buf[position] = jnp.zeros_like(cached_buf[position])
            fresh_buf[position] = jnp.zeros_like(fresh_buf[position])

        return carry

    lax.fori_loop(0, last + 1, start, 0)

    def prepare(slot, carry):
        @pl.when(place_ref[slot] >= 0)
        def _():
            cosine, sine = query_cos_ref[slot], query_sin_ref[slot]
            heads = [
                turn(query_ref[slot, :, h * width : (h + 1) * width].astype(jnp.float32), cosine, sine)
                for h in range(group)
            ]
            turned[slot] = jnp.concatenate(heads, 0).astype(jnp.bfloat16)

        return carry

    lax.fori_loop(0, slots, prepare, 0)
    index = lax.broadcasted_iota(jnp.int32, (rows, span), 1)

    def wall(slot, position):
        limit = query_at_ref[slot] - position * span
        limit = jnp.concatenate([limit] * (span // width), 1)
        end = jnp.where(there(position), length_ref[position] - 1, -1)
        return jnp.where(index <= jnp.minimum(limit, end), 0.0, FAR)

    if stretches <= 4:
        for count in range(1, stretches + 1):

            @pl.when(last == count - 1)
            def _(count=count):
                for position in range(count):
                    copies(position, lambda copy: copy.wait())
                for position in range(count):
                    here = slice(position * span, (position + 1) * span)
                    keys_buf[here], values_buf[here] = ready(
                        cached_buf, fresh_buf, position, rows, tables
                    )

        def one(slot, carry):
            for count in range(1, stretches + 1):

                @pl.when(place_ref[slot] == count - 1)
                def _(count=count):
                    walls = [wall(slot, position) for position in range(count)]
                    walls = jnp.concatenate([jnp.concatenate(walls, 1)] * group, 0)
                    scores = score(turned[slot], keys_buf[: count * span]) + walls
                    highest = jnp.max(scores, 1, keepdims=True)
                    weight = jnp.exp2((scores - highest) * factor)
                    shape = top.shape[1:]
                    top[slot] = jnp.broadcast_to(highest, shape)
                    mass[slot] = jnp.broadcast_to(jnp.sum(weight, 1, keepdims=True), shape)
                    total[slot] = jnp.dot(
                        weight.astype(jnp.bfloat16),
                        values_buf[: count * span],
                        preferred_element_type=jnp.float32,
                    )

            return carry

        lax.fori_loop(0, slots, one, 0)
        return

    def stretch(position, carry):
        copies(position, lambda copy: copy.wait())
        keys_buf[:span], values_buf[:span] = ready(cached_buf, fresh_buf, position, rows, tables)

        def one(slot, carry):
            @pl.when(place_ref[slot] >= position)
            def _():
                walls = jnp.concatenate([wall(slot, position)] * group, 0)
                scores = score(turned[slot], keys_buf[:span]) + walls
                state = [ref.at[slot] for ref in (top, mass, total)]
                absorb(position == 0, state, scores, values_buf[:span], factor)

            return carry

        return lax.fori_loop(0, slots, one, carry)

    lax.fori_loop(0, last + 1, stretch, 0)


def late_body(pieces, locate, rows, factor, slot_ref, length_ref, place_ref, seq_ref, *refs):
    cached, fresh, refs = refs[:pieces], refs[pieces : 2 * pieces], refs[2 * pieces :]
    tables, (turned, early_top, early_mass, early_total, out_ref) = refs[:4], refs[4:9]
    top, mass, total, cached_buf, fresh_buf, sems = refs[9:]
    slots, _, columns = out_ref.shape
    span, width = cached_buf.shape[-2:]
    group = columns // width
    stretches = slot_ref.shape[0]
    last = functools.reduce(jnp.maximum, [place_ref[s] for s in range(slots)])

    def copies(position, act):
        places = locate(slot_ref[position], seq_ref[0], slots)
        places = [(wanted & (position < last), piece, index) for wanted, piece, index in places]
        fetch(act, places, cached, fresh, cached_buf, fresh_buf, sems, position)
        return functools.reduce(jnp.logical_or, [place[0] for place in places])

    if pieces:
        for position in range(stretches):
            copies(position, lambda copy: copy.start())
    for slot in range(slots):

        @pl.when(place_ref[slot] >= 0)
        def _(slot=slot):
            top[slot], mass[slot], total[slot] = early_top[slot], early_mass[slot], early_total[slot]

    def stretch(position, carry):
        @pl.when(copies(position, lambda copy: copy.wait()))
        def _():
            keys, values = ready(cached_buf, fresh_buf, position, rows, tables)
            index = lax.broadcasted_iota(jnp.int32, (1, span), 1)
            walls = jnp.where(index < length_ref[position], 0.0, FAR)
            for slot in range(slots):

                @pl.when(place_ref[slot] > position)
                def _(slot=slot):
                    scores = score(turned[slot], keys) + walls
                    absorb(False, [ref.at[slot] for ref in (top, mass, total)], scores, values, factor)

        return carry

    if pieces:
        lax.fori_loop(0, stretches, stretch, 0)
    for slot in range(slots):

        @pl.when(place_ref[slot] >= 0)
        def _(slot=slot):
            result = total[slot] / mass[slot]
            for head in range(group):
                mine = result[head * rows : (head + 1) * rows]
                out_ref[slot, :, head * width : (head + 1) * width] = mine.astype(jnp.bfloat16)

        @pl.when(place_ref[slot] < 0)
        def _(slot=slot):
            out_ref[slot] = jnp.zeros_like(out_ref[slot])


def attend(body, locate, lists, cached, fresh, near, out_shape, scratch, sizes, cost):
    rows, stretches, padded, span, width = sizes
    factor = width ** (-0.5) * math.log2(math.e)
    specs = [pl.BlockSpec(memory_space=SMEM)] * len(lists)
    specs += [pl.BlockSpec(memory_space=pl.ANY)] * (len(cached) + len(fresh))
    specs += [pl.BlockSpec(memory_space=VMEM)] * len(near)
    return pl.pallas_call(
        functools.partial(body, len(cached), locate, rows, factor),
        out_shape=out_shape,
        in_specs=specs,
        out_specs=jax.tree.map(lambda _: pl.BlockSpec(memory_space=VMEM), out_shape),
        scratch_shapes=[
            *scratch[0],
            pltpu.VMEM((stretches, 2, span, width), jnp.bfloat16),
            pltpu.VMEM((stretches, 2, padded, width), jnp.bfloat16),
            *scratch[1],
            pltpu.SemaphoreType.DMA((stretches, 2)),
        ],
        cost_estimate=pl.CostEstimate(flops=cost, bytes_accessed=1000, transcendentals=0),
        compiler_params=pltpu.CompilerParams(vmem_limit_bytes=32 << 20),
        name=body.__name__,
    )(*lists, *cached, *fresh, *near)


def locate_all(slot, seq, slots):
    return [(slot >= 0, 0, slot)]


def locate_early(slot, seq, slots):
    away = (slot // slots) ^ seq
    return [(away == k, k, slot % slots) for k in range(3)]


def locate_late(slot, seq, slots):
    return [((slot // slots) ^ seq == 3, 0, slot % slots)]


def local(
    pool_kv, hidden_rows, norm_gain, kv_weight, queries, stretch_slot, stretch_lengths, recompute_rows
):
    slots, _, span, width = pool_kv.shape
    rows = recompute_rows.shape[1]
    stretches = stretch_slot.shape[0]
    seq_count = lax.axis_size("seq")
    seq = lax.axis_index("seq")
    parts = lax.axis_size(FEATURES)
    me = lax.axis_index(FEATURES)
    features = hidden_rows.shape[2] * parts
    exchanged = seq_count == 4 and slots == 2
    padded = round_up(rows + 1, 16)

    def along_seq(value, distance):
        return lax.ppermute(value, "seq", [(z, z ^ distance) for z in range(seq_count)])

    if exchanged:
        across = along_seq(pool_kv, 2)
        beside = along_seq(pool_kv, 1)

    marks = jnp.pad(recompute_rows.astype(jnp.float32), ((0, 0), (0, width - rows)), constant_values=-1.0)

    pieces = project(me.reshape(1).astype(jnp.int32), hidden_rows, norm_gain, kv_weight, parts)
    sums = [pieces[0]]
    for distance in range(parts - 1, 0, -1):
        swap = [(i, i ^ distance) for i in range(parts)]
        sums.append(lax.ppermute(pieces[distance], FEATURES, swap))
    fresh_kv, payload = finish(sums, marks, slots, rows, width, features)

    mine = seq * slots + jnp.arange(slots, dtype=jnp.int32)
    hits = stretch_slot[:, None] == mine[None]
    order = jnp.arange(stretches, dtype=jnp.int32)[:, None]
    my_pos = jnp.max(jnp.where(hits, order, -1), 0)
    query_at = my_pos[:, None] * span + recompute_rows
    inverse = THETA ** (-2.0 * np.arange(width // 2) / width)
    inverse = np.concatenate([inverse, inverse]).astype(np.float32)
    angle = query_at.astype(jnp.float32)[..., None] * inverse
    flip = np.where(np.arange(width) < width // 2, -1.0, 1.0).astype(np.float32)
    query_tables = (
        jnp.broadcast_to(query_at[..., None], (slots, rows, width)),
        jnp.cos(angle),
        jnp.sin(angle) * flip,
    )
    tables = (*rope_tables(np.arange(span), width), *rope_tables(np.arange(stretches) * span, width))

    if exchanged:
        across = tie(across, [beside, payload])
        beyond = along_seq(across, 1)
        payloads = [payload, *[along_seq(payload, k) for k in (1, 2, 3)]]
        early, late = ([pool_kv, beside, across], payloads[:3]), ([beyond], payloads[3:])
        locate = locate_early
    else:
        early = [[lax.all_gather(array, "seq", axis=0, tiled=True)] for array in (pool_kv, payload)]
        late = ([], [])
        locate = locate_all

    lists = (stretch_slot, stretch_lengths, my_pos, seq.reshape(1))
    lines = rows * (queries.shape[2] // width)
    sizes = (rows, stretches, padded, span, width)
    state = jax.ShapeDtypeStruct((slots, lines, width), jnp.float32)
    held = pltpu.VMEM((slots, lines, width), jnp.float32)
    stage = pltpu.VMEM(((stretches if stretches <= 4 else 1) * span, width), jnp.bfloat16)
    passed = attend(
        early_body,
        locate,
        lists,
        *early,
        (queries, *query_tables, *tables),
        [jax.ShapeDtypeStruct((slots, lines, width), jnp.bfloat16), state, state, state],
        ([], [stage, stage]),
        sizes,
        10**10,
    )
    attended = attend(
        late_body,
        locate_late,
        lists,
        *late,
        (*tables, *passed),
        jax.ShapeDtypeStruct(queries.shape, jnp.bfloat16),
        ([held, held, held], []),
        sizes,
        1000,
    )
    return fresh_kv, attended


def solution(mesh):
    in_specs = (
        P(("groups", "seq"), None, None, FEATURES),
        P(("groups", "seq"), None, FEATURES),
        P(FEATURES),
        P(FEATURES, None),
        P(("groups", "seq"), None, FEATURES),
        P("groups"),
        P("groups"),
        P(("groups", "seq"), None),
    )
    out_specs = (
        P(("groups", "seq"), None, None, FEATURES),
        P(("groups", "seq"), None, FEATURES),
    )
    return jax.shard_map(local, mesh=mesh, in_specs=in_specs, out_specs=out_specs, check_vma=False)
```

time: 42.8 us -> 30.8 us (0.72)
  the two profiles are of different devices: /device:TPU:6 before, /device:TPU:0 now
where the time goes in v2:
time: 30.8 us; the launch traced here: 30.6 us
  starting transfers between devices  12.1 us (39%)
  waiting for transfers between devices  9.46 us (31%)
  Pallas kernels  6.83 us (22%)
  local copies, waits for them, and re-layouts  0.94 us (3%)
  between operations  0.83 us (3%)
  other arithmetic  0.49 us (2%)
    ppermute x6, starting transfers between devices, along_seq(): lax.ppermute(value, 'seq', [(z, z ^ distance) for z in range(seq_count)])  10.1 us
    ppermute x6, waiting for transfers between devices, along_seq(): lax.ppermute(value, 'seq', [(z, z ^ distance) for z in range(seq_count)])  6.49 us
    pallas_call x2, Pallas kernels, attend(): pl.pallas_call(functools.partial(body, len(cached), locate, rows, factor)...  3.32 us
    ppermute x3, waiting for transfers between devices, local(): sums.append(lax.ppermute(pieces[distance], FEATURES, swap))  2.97 us
    pallas_call x1, Pallas kernels, project(): pl.pallas_call(project_body, out_shape=[jax.ShapeDtypeStruct(shape, jnp.b...  2.79 us
    ppermute x3, starting transfers between devices, local(): sums.append(lax.ppermute(pieces[distance], FEATURES, swap))  1.93 us
    unnamed x24, local copies, waits for them, and re-layouts  0.86 us
    pallas_call x1, Pallas kernels, finish(): pl.pallas_call(functools.partial(finish_body, features), out_shape=[jax.S...  0.72 us
  transfers between devices with their start and end apart: 9, of which 4 were waited for; matrix products, arithmetic and copies ran while one was open for 2% of the time, Pallas kernels for 17%

profile of v2, /device:TPU:0, one launch (start us, length us, event | category | flops | bytes accessed | tf_op | source)
XLA Modules:
  0.0 30.6 jit_solution(9853187776651686821)
XLA Ops:
  0.6 0.0 copy-start.10
  0.6 0.0 copy-start.11
  0.7 0.0 copy-start
  0.8 3.1 %collective-permute-start.4 = (bf16[2,2,256,128]{3,2,1,0:T(8,128)(2,1)}, bf16[2,2,256,128]{3,2,1,0:T(8,128)(2,1)S(1)}, u32[]{:S(2)}, u32[]{:S(2)}) collective-permute-start(bf16[2,2,256,128]{3,2,1,0:T(8,128)(2,1)} %refs_0_.1), channel_id=1, source_target_pairs={{0,4},{4,0},{8,12},{12,8},{1,5},{5,1},{9,13},{13,9},{2,6},{6,2},{1... | collective-permute-start | bytes 786440 | tf_op jit(solution)/shard_map/ppermute | solution.py:424
  3.8 2.6 %collective-permute-start.3 = (bf16[2,2,256,128]{3,2,1,0:T(8,128)(2,1)}, bf16[2,2,256,128]{3,2,1,0:T(8,128)(2,1)S(1)}, u32[]{:S(2)}, u32[]{:S(2)}) collective-permute-start(bf16[2,2,256,128]{3,2,1,0:T(8,128)(2,1)} %refs_0_.1), channel_id=1, source_target_pairs={{0,8},{4,12},{8,0},{12,4},{1,9},{5,13},{9,1},{13,5},{2,10},{6,14},... | collective-permute-start | bytes 786440 | tf_op jit(solution)/shard_map/ppermute | solution.py:424
  6.4 2.8 %project.1 = (bf16[96,256]{1,0:T(8,128)(2,1)}, bf16[96,256]{1,0:T(8,128)(2,1)}, bf16[96,256]{1,0:T(8,128)(2,1)}, bf16[96,256]{1,0:T(8,128)(2,1)}) custom-call(s32[1]{0:T(128)} %bitcast.me_ref, bf16[2,40,1024]{2,1,0:T(8,128)(2,1)} %hidden_ref.1, bf16[1024]{0:T(1024)(128)(2,1)} %gain_ref.1, bf16[1024,1024]{1,0:T(8,128)(2,1)} %weight_ref.1), custom_call_target="tpu_custom_call" | custom-call | flops 1000 | bytes 1000 | tf_op jit(solution)/shard_map/project/pallas_call | solution.py:88
  9.2 0.4 %collective-permute-start = (bf16[96,256]{1,0:T(8,128)(2,1)}, bf16[96,256]{1,0:T(8,128)(2,1)S(1)}, u32[]{:S(2)}, u32[]{:S(2)}) collective-permute-start(bf16[96,256]{1,0:T(8,128)(2,1)} %get-tuple-element.13), channel_id=1, source_target_pairs={{0,3},{1,2},{2,1},{3,0},{4,7},{5,6},{6,5},{7,4},{8,11},{9,10},{10,... | collective-permute-start | bytes 147464 | tf_op jit(solution)/shard_map/ppermute | solution.py:436
  9.7 1.2 %collective-permute-start.1 = (bf16[96,256]{1,0:T(8,128)(2,1)}, bf16[96,256]{1,0:T(8,128)(2,1)S(1)}, u32[]{:S(2)}, u32[]{:S(2)}) collective-permute-start(bf16[96,256]{1,0:T(8,128)(2,1)} %get-tuple-element.14), channel_id=1, source_target_pairs={{0,2},{1,3},{2,0},{3,1},{4,6},{5,7},{6,4},{7,5},{8,10},{9,11},{10,... | collective-permute-start | bytes 147464 | tf_op jit(solution)/shard_map/ppermute | solution.py:436
  10.9 0.3 collective-permute-start.2
  11.2 0.2 fusion.1.place_ref
  11.4 0.1 fusion.2
  11.4 2.1 %collective-permute-done.refs_1_ = bf16[96,256]{1,0:T(8,128)(2,1)S(1)} collective-permute-done((bf16[96,256]{1,0:T(8,128)(2,1)}, bf16[96,256]{1,0:T(8,128)(2,1)S(1)}, u32[]{:S(2)}, u32[]{:S(2)}) %collective-permute-start) | collective-permute-done | bytes 49184 | tf_op jit(solution)/shard_map/ppermute | solution.py:436
  13.5 0.9 %collective-permute-done.1.refs_2_ = bf16[96,256]{1,0:T(8,128)(2,1)S(1)} collective-permute-done((bf16[96,256]{1,0:T(8,128)(2,1)}, bf16[96,256]{1,0:T(8,128)(2,1)S(1)}, u32[]{:S(2)}, u32[]{:S(2)}) %collective-permute-start.1) | collective-permute-done | bytes 49184 | tf_op jit(solution)/shard_map/ppermute | solution.py:436
  14.4 0.8 %copy-done.2 = bf16[96,256]{1,0:T(8,128)(2,1)S(1)} copy-done((bf16[96,256]{1,0:T(8,128)(2,1)S(1)}, bf16[96,256]{1,0:T(8,128)(2,1)}, u32[]{:S(2)}) %copy-start.2) | copy-done | bytes 49176
  15.2 0.7 %finish.1 = (bf16[2,2,40,128]{3,2,1,0:T(8,128)(2,1)}, bf16[2,2,48,128]{3,2,1,0:T(8,128)(2,1)S(1)}) custom-call(f32[2,128]{1,0:T(2,128)S(1)} %pad.4.marks_ref, bf16[96,256]{1,0:T(8,128)(2,1)S(1)} %copy-done.2, bf16[96,256]{1,0:T(8,128)(2,1)S(1)} %collective-permute-done.refs_1_, bf16[96,256]{1,0:T(8,128)(2,1)S(1)} %collective-permute-done.1.refs_2_, ...), custom_call_target="tpu_custom_call" | custom-call | flops 1000 | bytes 1000 | tf_op jit(solution)/shard_map/finish/pallas_call | solution.py:128
  15.9 0.5 %collective-permute-start.7 = (bf16[2,2,48,128]{3,2,1,0:T(8,128)(2,1)S(1)}, bf16[2,2,48,128]{3,2,1,0:T(8,128)(2,1)S(1)}, u32[]{:S(2)}, u32[]{:S(2)}) collective-permute-start(bf16[2,2,48,128]{3,2,1,0:T(8,128)(2,1)S(1)} %get-tuple-element.17.refs_2_.refs_3_), channel_id=1, source_target_pairs={{0,4},{4,0},{8,12},{12,8},{1,5},{5,1},{9,13},{13,9},{2,6},{6,2},{1... | collective-permute-start | bytes 147464 | tf_op jit(solution)/shard_map/ppermute | solution.py:424
  16.4 0.2 collective-permute-start.8
  16.6 0.2 fusion
  16.8 3.8 %collective-permute-start.6 = (bf16[2,2,48,128]{3,2,1,0:T(8,128)(2,1)S(1)}, bf16[2,2,48,128]{3,2,1,0:T(8,128)(2,1)S(1)}, u32[]{:S(2)}, u32[]{:S(2)}) collective-permute-start(bf16[2,2,48,128]{3,2,1,0:T(8,128)(2,1)S(1)} %get-tuple-element.17.refs_2_.refs_3_), channel_id=1, source_target_pairs={{0,12},{4,8},{8,4},{12,0},{1,13},{5,9},{9,5},{13,1},{2,14},{6,10},... | collective-permute-start | bytes 147464 | tf_op jit(solution)/shard_map/ppermute | solution.py:424
  20.7 2.6 %collective-permute-done.8.refs_5_ = bf16[2,2,48,128]{3,2,1,0:T(8,128)(2,1)S(1)} collective-permute-done((bf16[2,2,48,128]{3,2,1,0:T(8,128)(2,1)S(1)}, bf16[2,2,48,128]{3,2,1,0:T(8,128)(2,1)S(1)}, u32[]{:S(2)}, u32[]{:S(2)}) %collective-permute-start.8) | collective-permute-done | bytes 49184 | tf_op jit(solution)/shard_map/ppermute | solution.py:424
  23.3 0.1 broadcast_in_dim.16.refs_7_
  23.4 1.8 %early_body.1 = (bf16[2,320,128]{2,1,0:T(8,128)(2,1)S(1)}, f32[2,320,128]{2,1,0:T(8,128)S(1)}, f32[2,320,128]{2,1,0:T(8,128)S(1)}, f32[2,320,128]{2,1,0:T(8,128)S(1)}) custom-call(s32[4]{0:T(128)S(1)} %copy-done.5, s32[4]{0:T(128)S(1)} %copy-done.6, s32[2]{0:T(128)S(1)} %fusion.1.place_ref, s32[1]{0:T(128)} %bitcast.1.seq_ref, ...), custom_call_target="tpu_custom_call" | custom-call | flops 10000000000 | bytes 1000 | tf_op jit(solution)/shard_map/early_body/pallas_call | solution.py:378
  25.2 3.9 %collective-permute-done.5.refs_0_ = bf16[2,2,256,128]{3,2,1,0:T(8,128)(2,1)S(1)} collective-permute-done((bf16[2,2,256,128]{3,2,1,0:T(8,128)(2,1)S(1)}, bf16[2,2,256,128]{3,2,1,0:T(8,128)(2,1)S(1)}, u32[]{:S(2)}, u32[]{:S(2)}) %collective-permute-start.5) | collective-permute-done | bytes 262176 | tf_op jit(solution)/shard_map/ppermute | solution.py:424
  29.1 1.5 %late_body.1 = bf16[2,40,1024]{2,1,0:T(8,128)(2,1)} custom-call(s32[4]{0:T(128)S(1)} %copy-done.5, s32[4]{0:T(128)S(1)} %copy-done.6, s32[2]{0:T(128)S(1)} %fusion.1.place_ref, s32[1]{0:T(128)} %bitcast.1.seq_ref, bf16[2,2,256,128]{3,2,1,0:T(8,128)(2,1)S(1)} %collective-permute-done.5.refs_0_, bf16[2,2,48,128]{3,2,1,0:T(8,128)(2,1)S(1)} %collective-permute-done.6.refs_1_, ...), custom_call_target="tpu_custom_call" | custom-call | flops 1000 | bytes 1000 | tf_op jit(solution)/shard_map/late_body/pallas_call | solution.py:378
  (30 shorter events, 0.1 us)
Async XLA Ops:
  0.6 15.9 %copy-start.10 = (f32[128]{0:T(128)S(1)}, f32[128]{0:T(128)}, u32[]{:S(2)}) copy-start(f32[128]{0:T(128)} %constant.33.clone) | copy-start | bytes 1540
  0.6 15.9 %copy-start.11 = (f32[128]{0:T(128)S(1)}, f32[128]{0:T(128)}, u32[]{:S(2)}) copy-start(f32[128]{0:T(128)} %constant.34.clone) | copy-start | bytes 1540
  0.7 22.7 %copy-start = (f32[256,128]{1,0:T(8,128)S(1)}, f32[256,128]{1,0:T(8,128)}, u32[]{:S(2)}) copy-start(f32[256,128]{1,0:T(8,128)} %constant.35.clone.refs_10_.refs_2_) | copy-start | bytes 393220
  0.7 22.7 %copy-start.1 = (f32[256,128]{1,0:T(8,128)S(1)}, f32[256,128]{1,0:T(8,128)}, u32[]{:S(2)}) copy-start(f32[256,128]{1,0:T(8,128)} %constant.36.clone.refs_11_.refs_3_) | copy-start | bytes 393220
  0.7 22.7 %copy-start.3 = (f32[4,128]{1,0:T(4,128)S(1)}, f32[4,128]{1,0:T(4,128)}, u32[]{:S(2)}) copy-start(f32[4,128]{1,0:T(4,128)} %constant.37.clone.refs_12_.refs_4_) | copy-start | bytes 6148
  0.7 22.7 %copy-start.4 = (f32[4,128]{1,0:T(4,128)S(1)}, f32[4,128]{1,0:T(4,128)}, u32[]{:S(2)}) copy-start(f32[4,128]{1,0:T(4,128)} %constant.38.clone.refs_13_.refs_5_) | copy-start | bytes 6148
  0.7 22.7 %copy-start.7 = (bf16[2,2,256,128]{3,2,1,0:T(8,128)(2,1)S(1)}, bf16[2,2,256,128]{3,2,1,0:T(8,128)(2,1)}, u32[]{:S(2)}) copy-start(bf16[2,2,256,128]{3,2,1,0:T(8,128)(2,1)} %refs_0_.1) | copy-start | bytes 786436
  0.7 10.4 %copy-start.5 = (s32[4]{0:T(128)S(1)}, s32[4]{0:T(128)}, u32[]{:S(2)}) copy-start(s32[4]{0:T(128)} %slot_ref.3) | copy-start | bytes 52
  0.7 10.6 %copy-start.9 = (s32[2,40]{1,0:T(2,128)S(1)}, s32[2,40]{1,0:T(2,128)}, u32[]{:S(2)}) copy-start(s32[2,40]{1,0:T(2,128)} %param.21) | copy-start | bytes 964
  0.7 22.7 %copy-start.8 = (bf16[2,40,1024]{2,1,0:T(8,128)(2,1)S(1)}, bf16[2,40,1024]{2,1,0:T(8,128)(2,1)}, u32[]{:S(2)}) copy-start(bf16[2,40,1024]{2,1,0:T(8,128)(2,1)} %refs_6_.1) | copy-start | bytes 491524
  0.7 22.7 %copy-start.6 = (s32[4]{0:T(128)S(1)}, s32[4]{0:T(128)}, u32[]{:S(2)}) copy-start(s32[4]{0:T(128)} %length_ref.3) | copy-start | bytes 52
  0.8 19.9 %collective-permute-start.4 = (bf16[2,2,256,128]{3,2,1,0:T(8,128)(2,1)}, bf16[2,2,256,128]{3,2,1,0:T(8,128)(2,1)S(1)}, u32[]{:S(2)}, u32[]{:S(2)}) collective-permute-start(bf16[2,2,256,128]{3,2,1,0:T(8,128)(2,1)} %refs_0_.1), channel_id=1, source_target_pairs={{0,4},{4,0},{8,12},{12,8},{1,5},{5,1},{9,13},{13,9},{2,6},{6,2},{1... | collective-permute-start | bytes 786440 | tf_op jit(solution)/shard_map/ppermute | solution.py:424
  3.8 16.8 %collective-permute-start.3 = (bf16[2,2,256,128]{3,2,1,0:T(8,128)(2,1)}, bf16[2,2,256,128]{3,2,1,0:T(8,128)(2,1)S(1)}, u32[]{:S(2)}, u32[]{:S(2)}) collective-permute-start(bf16[2,2,256,128]{3,2,1,0:T(8,128)(2,1)} %refs_0_.1), channel_id=1, source_target_pairs={{0,8},{4,12},{8,0},{12,4},{1,9},{5,13},{9,1},{13,5},{2,10},{6,14},... | collective-permute-start | bytes 786440 | tf_op jit(solution)/shard_map/ppermute | solution.py:424
  9.2 4.3 %collective-permute-start = (bf16[96,256]{1,0:T(8,128)(2,1)}, bf16[96,256]{1,0:T(8,128)(2,1)S(1)}, u32[]{:S(2)}, u32[]{:S(2)}) collective-permute-start(bf16[96,256]{1,0:T(8,128)(2,1)} %get-tuple-element.13), channel_id=1, source_target_pairs={{0,3},{1,2},{2,1},{3,0},{4,7},{5,6},{6,5},{7,4},{8,11},{9,10},{10,... | collective-permute-start | bytes 147464 | tf_op jit(solution)/shard_map/ppermute | solution.py:436
  9.7 4.7 %collective-permute-start.1 = (bf16[96,256]{1,0:T(8,128)(2,1)}, bf16[96,256]{1,0:T(8,128)(2,1)S(1)}, u32[]{:S(2)}, u32[]{:S(2)}) collective-permute-start(bf16[96,256]{1,0:T(8,128)(2,1)} %get-tuple-element.14), channel_id=1, source_target_pairs={{0,2},{1,3},{2,0},{3,1},{4,6},{5,7},{6,4},{7,5},{8,10},{9,11},{10,... | collective-permute-start | bytes 147464 | tf_op jit(solution)/shard_map/ppermute | solution.py:436
  10.9 3.5 %collective-permute-start.2 = (bf16[96,256]{1,0:T(8,128)(2,1)}, bf16[96,256]{1,0:T(8,128)(2,1)S(1)}, u32[]{:S(2)}, u32[]{:S(2)}) collective-permute-start(bf16[96,256]{1,0:T(8,128)(2,1)} %get-tuple-element.15), channel_id=1, source_target_pairs={{0,1},{1,0},{2,3},{3,2},{4,5},{5,4},{6,7},{7,6},{8,9},{9,8},{10,11... | collective-permute-start | bytes 147464 | tf_op jit(solution)/shard_map/ppermute | solution.py:436
  14.4 0.8 %copy-start.2 = (bf16[96,256]{1,0:T(8,128)(2,1)S(1)}, bf16[96,256]{1,0:T(8,128)(2,1)}, u32[]{:S(2)}) copy-start(bf16[96,256]{1,0:T(8,128)(2,1)} %get-tuple-element.12.refs_0_) | copy-start | bytes 147460
  15.9 4.7 %collective-permute-start.7 = (bf16[2,2,48,128]{3,2,1,0:T(8,128)(2,1)S(1)}, bf16[2,2,48,128]{3,2,1,0:T(8,128)(2,1)S(1)}, u32[]{:S(2)}, u32[]{:S(2)}) collective-permute-start(bf16[2,2,48,128]{3,2,1,0:T(8,128)(2,1)S(1)} %get-tuple-element.17.refs_2_.refs_3_), channel_id=1, source_target_pairs={{0,4},{4,0},{8,12},{12,8},{1,5},{5,1},{9,13},{13,9},{2,6},{6,2},{1... | collective-permute-start | bytes 147464 | tf_op jit(solution)/shard_map/ppermute | solution.py:424
  16.4 6.9 %collective-permute-start.8 = (bf16[2,2,48,128]{3,2,1,0:T(8,128)(2,1)S(1)}, bf16[2,2,48,128]{3,2,1,0:T(8,128)(2,1)S(1)}, u32[]{:S(2)}, u32[]{:S(2)}) collective-permute-start(bf16[2,2,48,128]{3,2,1,0:T(8,128)(2,1)S(1)} %get-tuple-element.17.refs_2_.refs_3_), channel_id=1, source_target_pairs={{0,8},{4,12},{8,0},{12,4},{1,9},{5,13},{9,1},{13,5},{2,10},{6,14},... | collective-permute-start | bytes 147464 | tf_op jit(solution)/shard_map/ppermute | solution.py:424
  16.8 8.4 %collective-permute-start.6 = (bf16[2,2,48,128]{3,2,1,0:T(8,128)(2,1)S(1)}, bf16[2,2,48,128]{3,2,1,0:T(8,128)(2,1)S(1)}, u32[]{:S(2)}, u32[]{:S(2)}) collective-permute-start(bf16[2,2,48,128]{3,2,1,0:T(8,128)(2,1)S(1)} %get-tuple-element.17.refs_2_.refs_3_), channel_id=1, source_target_pairs={{0,12},{4,8},{8,4},{12,0},{1,13},{5,9},{9,5},{13,1},{2,14},{6,10},... | collective-permute-start | bytes 147464 | tf_op jit(solution)/shard_map/ppermute | solution.py:424
  20.6 8.4 %collective-permute-start.5 = (bf16[2,2,256,128]{3,2,1,0:T(8,128)(2,1)S(1)}, bf16[2,2,256,128]{3,2,1,0:T(8,128)(2,1)S(1)}, u32[]{:S(2)}, u32[]{:S(2)}) collective-permute-start(bf16[2,2,256,128]{3,2,1,0:T(8,128)(2,1)S(1)} %tie.1.refs_2_), channel_id=1, source_target_pairs={{0,4},{4,0},{8,12},{12,8},{1,5},{5,1},{9,13},{13,9},{2,6},{6,2},{1... | collective-permute-start | bytes 786440 | tf_op jit(solution)/shard_map/ppermute | solution.py:424

commit v3 on v2

--- a/solution.py
+++ b/solution.py
@@ -16,6 +16,7 @@
 VMEM = pltpu.MemorySpace.VMEM
 SMEM = pltpu.MemorySpace.SMEM
 PROJECT_VMEM = 61 << 20
+EARLY_COST = 3*10**9
 
 
 def round_up(value, step):
@@ -32,8 +33,27 @@
     return values * cosine + pltpu.roll(values, values.shape[-1] // 2, 1) * sine
 
 
+def place_of(slot, slot_ref):
+    place = jnp.int32(-1)
+    for position in range(slot_ref.shape[0]):
+        place = jnp.where(slot_ref[position] == slot, jnp.int32(position), place)
+    return place
+
+
+def outer(seq):
+    return jnp.where((seq == 0) | (seq == 3), 1, 0)
+
+
+def far_slots(seq, slot_ref):
+    last = jnp.maximum(*[place_of(2 * seq + j, slot_ref) for j in range(2)])
+    slots = [2 * (seq ^ 3) + j for j in range(2)]
+    slots = [jnp.where(place_of(slot, slot_ref) < last, slot, -1) for slot in slots]
+    slots = [jnp.where(place_of(slot, slot_ref) < 0, -1, slot) for slot in slots]
+    return [jnp.where(slots[0] >= 0, slots[0], slots[1]), jnp.where(slots[0] >= 0, slots[1], -1)]
+
+
 def project_body(me_ref, hidden_ref, gain_ref, weight_ref, *refs):
-    pieces, (held, gain, weights, whole, sems) = refs[:-5], refs[-5:]
+    *pieces, held, gain, weights, whole, sems = refs
     chunks, depth, width = weights.shape
     slots, rows, features = held.shape
     count = slots * rows
@@ -137,35 +157,61 @@
     )(marks, *pieces)
 
 
-def tie_body(*refs):
-    pass
-
-
-def tie(value, others):
+def assemble_body(seq_ref, one_ref, two_ref, ahead_ref, out_ref, sem):
+    del ahead_ref
+    at_end = outer(seq_ref[0])
+    for wanted, ref in ((0, one_ref), (1, two_ref)):
+
+        @pl.when(at_end == wanted)
+        def _(ref=ref):
+            copy = pltpu.make_async_copy(ref, out_ref, sem)
+            copy.start()
+            copy.wait()
+
+
+def assemble(seq, one, two, ahead):
+    far = pl.BlockSpec(memory_space=pl.ANY)
     return pl.pallas_call(
-        tie_body,
+        assemble_body,
+        out_shape=jax.ShapeDtypeStruct(one.shape, one.dtype),
+        in_specs=[pl.BlockSpec(memory_space=SMEM), far, far, far],
+        out_specs=pl.BlockSpec(memory_space=VMEM),
+        scratch_shapes=[pltpu.SemaphoreType.DMA(())],
+        cost_estimate=pl.CostEstimate(flops=1000, bytes_accessed=1000, transcendentals=0),
+        compiler_params=pltpu.CompilerParams(vmem_limit_bytes=8 << 20),
+        name="assemble",
+    )(seq, one, two, ahead)
+
+
+def hold_body(value_ref, *refs):
+    refs[-1][...] = value_ref[...]
+
+
+def hold(value, *ahead):
+    near, far = pl.BlockSpec(memory_space=VMEM), pl.BlockSpec(memory_space=pl.ANY)
+    return pl.pallas_call(
+        hold_body,
         out_shape=jax.ShapeDtypeStruct(value.shape, value.dtype),
-        in_specs=[pl.BlockSpec(memory_space=pl.ANY)] * (1 + len(others)),
-        out_specs=pl.BlockSpec(memory_space=pl.ANY),
-        input_output_aliases={0: 0},
+        in_specs=[near] + [far] * len(ahead),
+        out_specs=near,
         cost_estimate=pl.CostEstimate(flops=1000, bytes_accessed=1000, transcendentals=0),
-        compiler_params=pltpu.CompilerParams(vmem_limit_bytes=1 << 20),
-        name="tie",
-    )(value, *others)
-
-
-def ready(cached_buf, fresh_buf, position, rows, tables):
+        compiler_params=pltpu.CompilerParams(vmem_limit_bytes=8 << 20),
+        name="hold",
+    )(value, *ahead)
+
+
+def ready(cached, fresh, position, rows, tables):
     cos_ref, sin_ref, base_cos_ref, base_sin_ref = tables
-    span, width = cached_buf.shape[-2:]
+    _, span, width = cached.shape
     start = rows - rows % 16
-    marks = fresh_buf[position, 0, start:].astype(jnp.float32)[rows - start : rows - start + 1]
+    marks = fresh[0, start:].astype(jnp.float32)[rows - start : rows - start + 1]
     token = lax.broadcasted_iota(jnp.int32, (span, width), 0).astype(jnp.float32)
-    chosen = jnp.where(token == marks, 1.0, 0.0).astype(jnp.bfloat16)[:, : fresh_buf.shape[-2]]
-    keys, values = fresh_buf[position, 0], fresh_buf[position, 1]
+    chosen = jnp.where(token == marks, 1.0, 0.0).astype(jnp.bfloat16)[:, : fresh.shape[-2]]
+    keys, values = fresh[0], fresh[1]
     source = jnp.concatenate([keys, values, jnp.ones_like(keys)], 1)
     placed = jnp.dot(chosen, source, preferred_element_type=jnp.float32)
     replaced = placed[:, 2 * width :] > 0.5
-    old_keys, old_values = cached_buf[position, 0], cached_buf[position, 1]
+    old_keys, old_values = cached[0], cached[1]
     keys = jnp.where(replaced, placed[:, :width], old_keys.astype(jnp.float32))
     values = jnp.where(replaced, placed[:, width : 2 * width], old_values.astype(jnp.float32))
     base_cos, base_sin = base_cos_ref[pl.ds(position, 1)], base_sin_ref[pl.ds(position, 1)]
@@ -176,11 +222,12 @@
 
 
 def fetch(act, places, cached, fresh, cached_buf, fresh_buf, sems, position):
-    for wanted, piece, index in places:
+    for wanted, *sources in places:
 
         @pl.when(wanted)
-        def _(piece=piece, index=index):
+        def _(sources=sources):
             for which, refs, buf in ((0, cached, cached_buf), (1, fresh, fresh_buf)):
+                piece, index = sources[which]
                 act(
                     pltpu.make_async_copy(
                         refs[piece].at[index], buf.at[position], sems.at[position, which]
@@ -217,11 +264,11 @@
     last = functools.reduce(jnp.maximum, [place_ref[s] for s in range(slots)])
 
     def there(position):
-        places = locate(slot_ref[position], seq_ref[0], slots)
+        places = locate(slot_ref[position], seq_ref[0], slot_ref)
         return functools.reduce(jnp.logical_or, [place[0] for place in places])
 
     def copies(position, act):
-        places = locate(slot_ref[position], seq_ref[0], slots)
+        places = locate(slot_ref[position], seq_ref[0], slot_ref)
         fetch(act, places, cached, fresh, cached_buf, fresh_buf, sems, position)
 
     def start(position, carry):
@@ -267,7 +314,7 @@
                 for position in range(count):
                     here = slice(position * span, (position + 1) * span)
                     keys_buf[here], values_buf[here] = ready(
-                        cached_buf, fresh_buf, position, rows, tables
+                        cached_buf.at[position], fresh_buf.at[position], position, rows, tables
                     )
 
         def one(slot, carry):
@@ -296,7 +343,9 @@
 
     def stretch(position, carry):
         copies(position, lambda copy: copy.wait())
-        keys_buf[:span], values_buf[:span] = ready(cached_buf, fresh_buf, position, rows, tables)
+        keys_buf[:span], values_buf[:span] = ready(
+            cached_buf.at[position], fresh_buf.at[position], position, rows, tables
+        )
 
         def one(slot, carry):
             @pl.when(place_ref[slot] >= position)
@@ -313,97 +362,94 @@
     lax.fori_loop(0, last + 1, stretch, 0)
 
 
-def late_body(pieces, locate, rows, factor, slot_ref, length_ref, place_ref, seq_ref, *refs):
-    cached, fresh, refs = refs[:pieces], refs[pieces : 2 * pieces], refs[2 * pieces :]
-    tables, (turned, early_top, early_mass, early_total, out_ref) = refs[:4], refs[4:9]
-    top, mass, total, cached_buf, fresh_buf, sems = refs[9:]
+def late_body(exchanged, rows, factor, slot_ref, length_ref, place_ref, seq_ref, *refs):
+    if exchanged:
+        message, fresh, *tables = refs[:6]
+        refs = refs[6:]
+    query_at_ref, turned, early_top, early_mass, early_total, out_ref, keys_buf, values_buf = refs
     slots, _, columns = out_ref.shape
-    span, width = cached_buf.shape[-2:]
+    width = turned.shape[-1]
     group = columns // width
-    stretches = slot_ref.shape[0]
-    last = functools.reduce(jnp.maximum, [place_ref[s] for s in range(slots)])
-
-    def copies(position, act):
-        places = locate(slot_ref[position], seq_ref[0], slots)
-        places = [(wanted & (position < last), piece, index) for wanted, piece, index in places]
-        fetch(act, places, cached, fresh, cached_buf, fresh_buf, sems, position)
-        return functools.reduce(jnp.logical_or, [place[0] for place in places])
-
-    if pieces:
-        for position in range(stretches):
-            copies(position, lambda copy: copy.start())
+
+    def write(slot, result):
+        for head in range(group):
+            mine = result[head * rows : (head + 1) * rows]
+            out_ref[slot, :, head * width : (head + 1) * width] = mine.astype(jnp.bfloat16)
+
+    def plain(slot):
+        write(slot, early_total[slot] / early_mass[slot])
+
     for slot in range(slots):
-
-        @pl.when(place_ref[slot] >= 0)
-        def _(slot=slot):
-            top[slot], mass[slot], total[slot] = early_top[slot], early_mass[slot], early_total[slot]
-
-    def stretch(position, carry):
-        @pl.when(copies(position, lambda copy: copy.wait()))
-        def _():
-            keys, values = ready(cached_buf, fresh_buf, position, rows, tables)
-            index = lax.broadcasted_iota(jnp.int32, (1, span), 1)
-            walls = jnp.where(index < length_ref[position], 0.0, FAR)
-            for slot in range(slots):
-
-                @pl.when(place_ref[slot] > position)
-                def _(slot=slot):
-                    scores = score(turned[slot], keys) + walls
-                    absorb(False, [ref.at[slot] for ref in (top, mass, total)], scores, values, factor)
-
-        return carry
-
-    if pieces:
-        lax.fori_loop(0, stretches, stretch, 0)
-    for slot in range(slots):
-
-        @pl.when(place_ref[slot] >= 0)
-        def _(slot=slot):
-            result = total[slot] / mass[slot]
-            for head in range(group):
-                mine = result[head * rows : (head + 1) * rows]
-                out_ref[slot, :, head * width : (head + 1) * width] = mine.astype(jnp.bfloat16)
 
         @pl.when(place_ref[slot] < 0)
         def _(slot=slot):
             out_ref[slot] = jnp.zeros_like(out_ref[slot])
 
-
-def attend(body, locate, lists, cached, fresh, near, out_shape, scratch, sizes, cost):
-    rows, stretches, padded, span, width = sizes
-    factor = width ** (-0.5) * math.log2(math.e)
+    if not exchanged:
+        for slot in range(slots):
+            pl.when(place_ref[slot] >= 0)(functools.partial(plain, slot))
+        return
+
+    _, _, span, _ = message.shape
+    seq = seq_ref[0]
+    chosen = far_slots(seq, slot_ref)
+    places = [place_of(slot, slot_ref) for slot in chosen]
+    for k, slot in enumerate(chosen):
+        @pl.when(slot >= 0)
+        def _(k=k, slot=slot):
+            keys_buf[k], values_buf[k] = ready(
+                message.at[slot % 2], fresh.at[slot % 2], places[k], rows, tables
+            )
+
+    index = lax.broadcasted_iota(jnp.int32, (1, span), 1)
+
+    def settle(slot, count):
+        scores = []
+        for k in range(count):
+            end = jnp.where(places[k] < place_ref[slot], length_ref[places[k]], 0)
+            scores.append(score(turned[slot], keys_buf[k]) + jnp.where(index < end, 0.0, FAR))
+        scores = jnp.concatenate(scores, 1)
+        before = early_top[slot]
+        after = jnp.maximum(before, jnp.max(scores, 1, keepdims=True))
+        fade = jnp.exp2((before - after) * factor)
+        weight = jnp.exp2((scores - after[:, :1]) * factor)
+        mass = early_mass[slot] * fade + jnp.sum(weight, 1, keepdims=True)
+        values = values_buf[:count].reshape(count * span, width)
+        added = jnp.dot(weight.astype(jnp.bfloat16), values, preferred_element_type=jnp.float32)
+        write(slot, (early_total[slot] * fade + added) / mass)
+
+    count = jnp.where(chosen[1] >= 0, 2, jnp.where(chosen[0] >= 0, 1, 0))
+    for slot in range(slots):
+        for cases, act in ((0, plain), (1, functools.partial(settle, count=1)), (2, functools.partial(settle, count=2))):
+            pl.when((place_ref[slot] >= 0) & (count == cases))(functools.partial(act, slot))
+
+
+def attend(body, lists, far, near, out_shape, scratch, cost):
     specs = [pl.BlockSpec(memory_space=SMEM)] * len(lists)
-    specs += [pl.BlockSpec(memory_space=pl.ANY)] * (len(cached) + len(fresh))
+    specs += [pl.BlockSpec(memory_space=pl.ANY)] * len(far)
     specs += [pl.BlockSpec(memory_space=VMEM)] * len(near)
     return pl.pallas_call(
-        functools.partial(body, len(cached), locate, rows, factor),
+        body,
         out_shape=out_shape,
         in_specs=specs,
         out_specs=jax.tree.map(lambda _: pl.BlockSpec(memory_space=VMEM), out_shape),
-        scratch_shapes=[
-            *scratch[0],
-            pltpu.VMEM((stretches, 2, span, width), jnp.bfloat16),
-            pltpu.VMEM((stretches, 2, padded, width), jnp.bfloat16),
-            *scratch[1],
-            pltpu.SemaphoreType.DMA((stretches, 2)),
-        ],
+        scratch_shapes=scratch,
         cost_estimate=pl.CostEstimate(flops=cost, bytes_accessed=1000, transcendentals=0),
         compiler_params=pltpu.CompilerParams(vmem_limit_bytes=32 << 20),
-        name=body.__name__,
-    )(*lists, *cached, *fresh, *near)
-
-
-def locate_all(slot, seq, slots):
-    return [(slot >= 0, 0, slot)]
-
-
-def locate_early(slot, seq, slots):
-    away = (slot // slots) ^ seq
-    return [(away == k, k, slot % slots) for k in range(3)]
-
-
-def locate_late(slot, seq, slots):
-    return [((slot // slots) ^ seq == 3, 0, slot % slots)]
+        name=body.func.__name__,
+    )(*lists, *far, *near)
+
+
+def locate_all(slot, seq, slot_ref):
+    return [(slot >= 0, (0, slot), (0, slot))]
+
+
+def locate_early(slot, seq, slot_ref):
+    away, index = (slot // 2) ^ seq, slot % 2
+    at_end = outer(seq)
+    near = [((away == 1) & (at_end == k), (2 - k, index), (1, index)) for k in range(2)]
+    next_but_one = [((away == 2) & (at_end == k), (1 + k, index), (2, index)) for k in range(2)]
+    return [(away == 0, (0, index), (0, index))] + near + next_but_one
 
 
 def local(
@@ -417,20 +463,21 @@
     parts = lax.axis_size(FEATURES)
     me = lax.axis_index(FEATURES)
     features = hidden_rows.shape[2] * parts
-    exchanged = seq_count == 4 and slots == 2
+    exchanged = seq_count == 4 and slots == 2 and stretches <= 4
     padded = round_up(rows + 1, 16)
 
     def along_seq(value, distance):
         return lax.ppermute(value, "seq", [(z, z ^ distance) for z in range(seq_count)])
 
+    first, second = [(0, 2), (3, 1), (1, 0), (2, 3)], [(1, 3), (2, 0), (0, 1), (3, 2)]
+
     if exchanged:
-        across = along_seq(pool_kv, 2)
-        beside = along_seq(pool_kv, 1)
+        one, two = [lax.ppermute(pool_kv, "seq", pairs) for pairs in (first, second)]
 
     marks = jnp.pad(recompute_rows.astype(jnp.float32), ((0, 0), (0, width - rows)), constant_values=-1.0)
 
-    pieces = project(me.reshape(1).astype(jnp.int32), hidden_rows, norm_gain, kv_weight, parts)
-    sums = [pieces[0]]
+    pieces = project(me.reshape(1), hidden_rows, norm_gain, kv_weight, parts)
+    sums = [hold(pieces[0])]
     for distance in range(parts - 1, 0, -1):
         swap = [(i, i ^ distance) for i in range(parts)]
         sums.append(lax.ppermute(pieces[distance], FEATURES, swap))
@@ -453,42 +500,44 @@
     tables = (*rope_tables(np.arange(span), width), *rope_tables(np.arange(stretches) * span, width))
 
     if exchanged:
-        across = tie(across, [beside, payload])
-        beyond = along_seq(across, 1)
-        payloads = [payload, *[along_seq(payload, k) for k in (1, 2, 3)]]
-        early, late = ([pool_kv, beside, across], payloads[:3]), ([beyond], payloads[3:])
-        locate = locate_early
+        payloads = [payload, along_seq(payload, 1), along_seq(payload, 2)]
+        message = assemble(seq.reshape(1), one, two, payload)
+        early, locate = ([pool_kv, one, two], payloads), locate_early
+        late = (along_seq(message, 1), along_seq(hold(payloads[2], message), 1), *tables)
     else:
         early = [[lax.all_gather(array, "seq", axis=0, tiled=True)] for array in (pool_kv, payload)]
-        late = ([], [])
-        locate = locate_all
+        locate, late = locate_all, ()
 
     lists = (stretch_slot, stretch_lengths, my_pos, seq.reshape(1))
     lines = rows * (queries.shape[2] // width)
-    sizes = (rows, stretches, padded, span, width)
-    state = jax.ShapeDtypeStruct((slots, lines, width), jnp.float32)
-    held = pltpu.VMEM((slots, lines, width), jnp.float32)
+    factor = width ** (-0.5) * math.log2(math.e)
+    state = (slots, lines, width)
     stage = pltpu.VMEM(((stretches if stretches <= 4 else 1) * span, width), jnp.bfloat16)
     passed = attend(
-        early_body,
-        locate,
+        functools.partial(early_body, len(early[0]), locate, rows, factor),
         lists,
-        *early,
+        (*early[0], *early[1]),
         (queries, *query_tables, *tables),
-        [jax.ShapeDtypeStruct((slots, lines, width), jnp.bfloat16), state, state, state],
-        ([], [stage, stage]),
-        sizes,
-        10**10,
+        [jax.ShapeDtypeStruct(state, jnp.bfloat16)] + [jax.ShapeDtypeStruct(state, jnp.float32)] * 3,
+        [
+            pltpu.VMEM((stretches, 2, span, width), jnp.bfloat16),
+            pltpu.VMEM((stretches, 2, padded, width), jnp.bfloat16),
+            stage,
+            stage,
+            pltpu.SemaphoreType.DMA((stretches, 2)),
+        ],
+        EARLY_COST,
     )
     attended = attend(
-        late_body,
-        locate_late,
+        functools.partial(late_body, exchanged, rows, factor),
         lists,
-        *late,
-        (*tables, *passed),
+        (),
+        (*late, query_tables[0], *passed),
         jax.ShapeDtypeStruct(queries.shape, jnp.bfloat16),
-        ([held, held, held], []),
-        sizes,
+        [
+            pltpu.VMEM((2, span, width), jnp.bfloat16),
+            pltpu.VMEM((2, span, width), jnp.bfloat16),
+        ],
         1000,
     )
     return fresh_kv, attended

time: 30.8 us -> 29.9 us (0.971)
  Pallas kernels: 6.83 us -> 9.08 us
  waiting for transfers between devices: 9.46 us -> 7.66 us
  starting transfers between devices: 12.1 us -> 10.9 us
    ppermute x6 -> x4, starting transfers between devices: 10.1 us -> 4.88 us  [along_seq(): lax.ppermute(value, 'seq', [(z, z ^ distance) for z in range(seq_count)])]
    ppermute x0 -> x2, starting transfers between devices: none -> 4.09 us  [local(): lax.ppermute(pool_kv, 'seq', pairs)]
    pallas_call x3 -> x5, Pallas kernels: 3.32 us -> 5.56 us  [the longest x2 5.53 us: attend(): pl.pallas_call(body, out_shape=out_shape, in_specs=specs, out_specs=jax.t...]
    ppermute x6 -> x4, waiting for transfers between devices: 6.49 us -> 4.42 us  [along_seq(): lax.ppermute(value, 'seq', [(z, z ^ distance) for z in range(seq_count)])]
    ppermute x0 -> x2, waiting for transfers between devices: none -> 0.73 us  [local(): lax.ppermute(pool_kv, 'seq', pairs)]
    ppermute x3, waiting for transfers between devices: 2.97 us -> 2.51 us  [local(): sums.append(lax.ppermute(pieces[distance], FEATURES, swap))]
  transfers between devices with their start and end apart: 9 -> 9, of which waited for: 4 -> 5; matrix products, arithmetic and copies ran while one was open for 2% -> 2% of each run, Pallas kernels for 17% -> 22%
where the time goes in v3:
time: 29.9 us
  starting transfers between devices  10.9 us (36%)
  Pallas kernels  9.08 us (30%)
  waiting for transfers between devices  7.66 us (26%)
  local copies, waits for them, and re-layouts  0.94 us (3%)
  between operations  0.83 us (3%)
  other arithmetic  0.49 us (2%)
    pallas_call x2, Pallas kernels, attend(): pl.pallas_call(body, out_shape=out_shape, in_specs=specs, out_specs=jax.t...  5.53 us
    ppermute x4, starting transfers between devices, along_seq(): lax.ppermute(value, 'seq', [(z, z ^ distance) for z in range(seq_count)])  4.88 us
    ppermute x4, waiting for transfers between devices, along_seq(): lax.ppermute(value, 'seq', [(z, z ^ distance) for z in range(seq_count)])  4.42 us
    ppermute x2, starting transfers between devices, local(): lax.ppermute(pool_kv, 'seq', pairs)  4.09 us
    pallas_call x1, Pallas kernels, project(): pl.pallas_call(project_body, out_shape=[jax.ShapeDtypeStruct(shape, jnp.b...  2.79 us
    ppermute x3, waiting for transfers between devices, local(): sums.append(lax.ppermute(pieces[distance], FEATURES, swap))  2.51 us
    ppermute x3, starting transfers between devices, local(): sums.append(lax.ppermute(pieces[distance], FEATURES, swap))  1.93 us
    unnamed x24, local copies, waits for them, and re-layouts  0.86 us
  transfers between devices with their start and end apart: 9, of which 5 were waited for; matrix products, arithmetic and copies ran while one was open for 2% of the time, Pallas kernels for 22%

profile of v3, /device:TPU:0, one launch (start us, length us, event | category | flops | bytes accessed | tf_op | source)
XLA Modules:
  0.0 29.9 jit_solution(2468217387539078406)
XLA Ops:
  0.6 0.0 copy-start.11
  0.7 0.0 copy-start
  0.8 4.1 %collective-permute-start.3 = (bf16[2,2,256,128]{3,2,1,0:T(8,128)(2,1)}, bf16[2,2,256,128]{3,2,1,0:T(8,128)(2,1)S(1)}, u32[]{:S(2)}, u32[]{:S(2)}) collective-permute-start(bf16[2,2,256,128]{3,2,1,0:T(8,128)(2,1)} %refs_0_.1), channel_id=1, source_target_pairs={{0,8},{12,4},{4,0},{8,12},{1,9},{13,5},{5,1},{9,13},{2,10},{14,6},... | collective-permute-start | bytes 786440 | tf_op jit(solution)/shard_map/ppermute | solution.py:475
  4.9 2.8 %project.1 = (bf16[96,256]{1,0:T(8,128)(2,1)}, bf16[96,256]{1,0:T(8,128)(2,1)}, bf16[96,256]{1,0:T(8,128)(2,1)}, bf16[96,256]{1,0:T(8,128)(2,1)}) custom-call(s32[1]{0:T(128)} %bitcast.me_ref, bf16[2,40,1024]{2,1,0:T(8,128)(2,1)} %hidden_ref.1, bf16[1024]{0:T(1024)(128)(2,1)} %gain_ref.1, bf16[1024,1024]{1,0:T(8,128)(2,1)} %weight_ref.1), custom_call_target="tpu_custom_call" | custom-call | flops 1000 | bytes 1000 | tf_op jit(solution)/shard_map/project/pallas_call | solution.py:108
  7.6 0.7 %collective-permute-start = (bf16[96,256]{1,0:T(8,128)(2,1)}, bf16[96,256]{1,0:T(8,128)(2,1)S(1)}, u32[]{:S(2)}, u32[]{:S(2)}) collective-permute-start(bf16[96,256]{1,0:T(8,128)(2,1)} %get-tuple-element.13), channel_id=1, source_target_pairs={{0,3},{1,2},{2,1},{3,0},{4,7},{5,6},{6,5},{7,4},{8,11},{9,10},{10,... | collective-permute-start | bytes 147464 | tf_op jit(solution)/shard_map/ppermute | solution.py:483
  8.4 0.9 %collective-permute-start.1 = (bf16[96,256]{1,0:T(8,128)(2,1)}, bf16[96,256]{1,0:T(8,128)(2,1)S(1)}, u32[]{:S(2)}, u32[]{:S(2)}) collective-permute-start(bf16[96,256]{1,0:T(8,128)(2,1)} %get-tuple-element.14), channel_id=1, source_target_pairs={{0,2},{1,3},{2,0},{3,1},{4,6},{5,7},{6,4},{7,5},{8,10},{9,11},{10,... | collective-permute-start | bytes 147464 | tf_op jit(solution)/shard_map/ppermute | solution.py:483
  9.3 0.3 collective-permute-start.2
  9.6 0.2 fusion.1.place_ref
  9.8 0.1 fusion.2
  9.9 0.8 %copy-done.2 = bf16[96,256]{1,0:T(8,128)(2,1)S(1)} copy-done((bf16[96,256]{1,0:T(8,128)(2,1)S(1)}, bf16[96,256]{1,0:T(8,128)(2,1)}, u32[]{:S(2)}) %copy-start.2) | copy-done | bytes 49176
  10.7 1.2 %collective-permute-done.refs_1_ = bf16[96,256]{1,0:T(8,128)(2,1)S(1)} collective-permute-done((bf16[96,256]{1,0:T(8,128)(2,1)}, bf16[96,256]{1,0:T(8,128)(2,1)S(1)}, u32[]{:S(2)}, u32[]{:S(2)}) %collective-permute-start) | collective-permute-done | bytes 49184 | tf_op jit(solution)/shard_map/ppermute | solution.py:483
  11.9 1.3 %collective-permute-done.1.refs_2_ = bf16[96,256]{1,0:T(8,128)(2,1)S(1)} collective-permute-done((bf16[96,256]{1,0:T(8,128)(2,1)}, bf16[96,256]{1,0:T(8,128)(2,1)S(1)}, u32[]{:S(2)}, u32[]{:S(2)}) %collective-permute-start.1) | collective-permute-done | bytes 49184 | tf_op jit(solution)/shard_map/ppermute | solution.py:483
  13.2 0.7 %finish.1 = (bf16[2,2,40,128]{3,2,1,0:T(8,128)(2,1)}, bf16[2,2,48,128]{3,2,1,0:T(8,128)(2,1)S(1)}) custom-call(f32[2,128]{1,0:T(2,128)S(1)} %pad.4.marks_ref, bf16[96,256]{1,0:T(8,128)(2,1)S(1)} %hold.2.refs_0_, bf16[96,256]{1,0:T(8,128)(2,1)S(1)} %collective-permute-done.refs_1_, bf16[96,256]{1,0:T(8,128)(2,1)S(1)} %collective-permute-done.1.refs_2_, ...), custom_call_target="tpu_custom_call" | custom-call | flops 1000 | bytes 1000 | tf_op jit(solution)/shard_map/finish/pallas_call | solution.py:148
  13.9 2.6 %collective-permute-start.6 = (bf16[2,2,48,128]{3,2,1,0:T(8,128)(2,1)S(1)}, bf16[2,2,48,128]{3,2,1,0:T(8,128)(2,1)S(1)}, u32[]{:S(2)}, u32[]{:S(2)}) collective-permute-start(bf16[2,2,48,128]{3,2,1,0:T(8,128)(2,1)S(1)} %get-tuple-element.17.ahead_ref.refs_3_), channel_id=1, source_target_pairs={{0,8},{4,12},{8,0},{12,4},{1,9},{5,13},{9,1},{13,5},{2,10},{6,14},... | collective-permute-start | bytes 147464 | tf_op jit(solution)/shard_map/ppermute | solution.py:470
  16.5 0.7 %collective-permute-start.8 = (bf16[2,2,48,128]{3,2,1,0:T(8,128)(2,1)S(1)}, bf16[2,2,48,128]{3,2,1,0:T(8,128)(2,1)S(1)}, u32[]{:S(2)}, u32[]{:S(2)}) collective-permute-start(bf16[2,2,48,128]{3,2,1,0:T(8,128)(2,1)S(1)} %get-tuple-element.17.ahead_ref.refs_3_), channel_id=1, source_target_pairs={{0,4},{4,0},{8,12},{12,8},{1,5},{5,1},{9,13},{13,9},{2,6},{6,2},{1... | collective-permute-start | bytes 147464 | tf_op jit(solution)/shard_map/ppermute | solution.py:470
  17.2 0.2 fusion
  17.4 0.7 %collective-permute-done.4.two_ref.refs_2_ = bf16[2,2,256,128]{3,2,1,0:T(8,128)(2,1)S(1)} collective-permute-done((bf16[2,2,256,128]{3,2,1,0:T(8,128)(2,1)}, bf16[2,2,256,128]{3,2,1,0:T(8,128)(2,1)S(1)}, u32[]{:S(2)}, u32[]{:S(2)}) %collective-permute-start.4) | collective-permute-done | bytes 262176 | tf_op jit(solution)/shard_map/ppermute | solution.py:475
  18.2 0.7 %collective-permute-start.5 = (bf16[2,2,256,128]{3,2,1,0:T(8,128)(2,1)S(1)}, bf16[2,2,256,128]{3,2,1,0:T(8,128)(2,1)S(1)}, u32[]{:S(2)}, u32[]{:S(2)}) collective-permute-start(bf16[2,2,256,128]{3,2,1,0:T(8,128)(2,1)S(1)} %assemble.1.refs_0_), channel_id=1, source_target_pairs={{0,4},{4,0},{8,12},{12,8},{1,5},{5,1},{9,13},{13,9},{2,6},{6,2},{1... | collective-permute-start | bytes 786440 | tf_op jit(solution)/shard_map/ppermute | solution.py:470
  18.9 1.0 %collective-permute-done.6.value_ref.refs_5_ = bf16[2,2,48,128]{3,2,1,0:T(8,128)(2,1)S(1)} collective-permute-done((bf16[2,2,48,128]{3,2,1,0:T(8,128)(2,1)S(1)}, bf16[2,2,48,128]{3,2,1,0:T(8,128)(2,1)S(1)}, u32[]{:S(2)}, u32[]{:S(2)}) %collective-permute-start.6) | collective-permute-done | bytes 49184 | tf_op jit(solution)/shard_map/ppermute | solution.py:470
  19.9 0.9 %collective-permute-start.7 = (bf16[2,2,48,128]{3,2,1,0:T(8,128)(2,1)S(1)}, bf16[2,2,48,128]{3,2,1,0:T(8,128)(2,1)S(1)}, u32[]{:S(2)}, u32[]{:S(2)}) collective-permute-start(bf16[2,2,48,128]{3,2,1,0:T(8,128)(2,1)S(1)} %hold.3), channel_id=1, source_target_pairs={{0,4},{4,0},{8,12},{12,8},{1,5},{5,1},{9,13},{13,9},{2,6},{6,2},{1... | collective-permute-start | bytes 147464 | tf_op jit(solution)/shard_map/ppermute | solution.py:470
  20.9 0.1 broadcast_in_dim.16.refs_7_.refs_6_
  21.0 3.1 %early_body.1 = (bf16[2,320,128]{2,1,0:T(8,128)(2,1)S(1)}, f32[2,320,128]{2,1,0:T(8,128)S(1)}, f32[2,320,128]{2,1,0:T(8,128)S(1)}, f32[2,320,128]{2,1,0:T(8,128)S(1)}) custom-call(s32[4]{0:T(128)S(1)} %copy-done.5, s32[4]{0:T(128)S(1)} %copy-done.6, s32[2]{0:T(128)S(1)} %fusion.1.place_ref, s32[1]{0:T(128)} %bitcast.1.seq_ref, ...), custom_call_target="tpu_custom_call" | custom-call | flops 3000000000 | bytes 1000 | tf_op jit(solution)/shard_map/early_body/pallas_call | solution.py:431
  24.1 3.4 %collective-permute-done.7.refs_1_ = bf16[2,2,48,128]{3,2,1,0:T(8,128)(2,1)S(1)} collective-permute-done((bf16[2,2,48,128]{3,2,1,0:T(8,128)(2,1)S(1)}, bf16[2,2,48,128]{3,2,1,0:T(8,128)(2,1)S(1)}, u32[]{:S(2)}, u32[]{:S(2)}) %collective-permute-start.7) | collective-permute-done | bytes 49184 | tf_op jit(solution)/shard_map/ppermute | solution.py:470
  27.4 2.5 %late_body.1 = bf16[2,40,1024]{2,1,0:T(8,128)(2,1)} custom-call(s32[4]{0:T(128)S(1)} %copy-done.5, s32[4]{0:T(128)S(1)} %copy-done.6, s32[2]{0:T(128)S(1)} %fusion.1.place_ref, s32[1]{0:T(128)} %bitcast.1.seq_ref, bf16[2,2,256,128]{3,2,1,0:T(8,128)(2,1)S(1)} %collective-permute-done.5.refs_0_, bf16[2,2,48,128]{3,2,1,0:T(8,128)(2,1)S(1)} %collective-permute-done.7.refs_1_, ...), custom_call_target="tpu_custom_call" | custom-call | flops 1000 | bytes 1000 | tf_op jit(solution)/shard_map/late_body/pallas_call | solution.py:431
  (32 shorter events, 0.1 us)
Async XLA Ops:
  0.6 16.5 %copy-start.10 = (f32[128]{0:T(128)S(1)}, f32[128]{0:T(128)}, u32[]{:S(2)}) copy-start(f32[128]{0:T(128)} %constant.33.clone) | copy-start | bytes 1540
  0.6 16.5 %copy-start.11 = (f32[128]{0:T(128)S(1)}, f32[128]{0:T(128)}, u32[]{:S(2)}) copy-start(f32[128]{0:T(128)} %constant.34.clone) | copy-start | bytes 1540
  0.7 20.3 %copy-start = (f32[256,128]{1,0:T(8,128)S(1)}, f32[256,128]{1,0:T(8,128)}, u32[]{:S(2)}) copy-start(f32[256,128]{1,0:T(8,128)} %constant.35.clone.refs_10_.refs_2_) | copy-start | bytes 393220
  0.7 20.3 %copy-start.1 = (f32[256,128]{1,0:T(8,128)S(1)}, f32[256,128]{1,0:T(8,128)}, u32[]{:S(2)}) copy-start(f32[256,128]{1,0:T(8,128)} %constant.36.clone.refs_11_.refs_3_) | copy-start | bytes 393220
  0.7 20.3 %copy-start.3 = (f32[4,128]{1,0:T(4,128)S(1)}, f32[4,128]{1,0:T(4,128)}, u32[]{:S(2)}) copy-start(f32[4,128]{1,0:T(4,128)} %constant.37.clone.refs_12_.refs_4_) | copy-start | bytes 6148
  0.7 20.3 %copy-start.4 = (f32[4,128]{1,0:T(4,128)S(1)}, f32[4,128]{1,0:T(4,128)}, u32[]{:S(2)}) copy-start(f32[4,128]{1,0:T(4,128)} %constant.38.clone.refs_13_.refs_5_) | copy-start | bytes 6148
  0.7 20.2 %copy-start.7 = (bf16[2,2,256,128]{3,2,1,0:T(8,128)(2,1)S(1)}, bf16[2,2,256,128]{3,2,1,0:T(8,128)(2,1)}, u32[]{:S(2)}) copy-start(bf16[2,2,256,128]{3,2,1,0:T(8,128)(2,1)} %refs_0_.1) | copy-start | bytes 786436
  0.7 8.9 %copy-start.5 = (s32[4]{0:T(128)S(1)}, s32[4]{0:T(128)}, u32[]{:S(2)}) copy-start(s32[4]{0:T(128)} %slot_ref.3) | copy-start | bytes 52
  0.7 9.0 %copy-start.9 = (s32[2,40]{1,0:T(2,128)S(1)}, s32[2,40]{1,0:T(2,128)}, u32[]{:S(2)}) copy-start(s32[2,40]{1,0:T(2,128)} %param.21) | copy-start | bytes 964
  0.7 20.2 %copy-start.8 = (bf16[2,40,1024]{2,1,0:T(8,128)(2,1)S(1)}, bf16[2,40,1024]{2,1,0:T(8,128)(2,1)}, u32[]{:S(2)}) copy-start(bf16[2,40,1024]{2,1,0:T(8,128)(2,1)} %refs_6_.1) | copy-start | bytes 491524
  0.7 20.2 %copy-start.6 = (s32[4]{0:T(128)S(1)}, s32[4]{0:T(128)}, u32[]{:S(2)}) copy-start(s32[4]{0:T(128)} %length_ref.3) | copy-start | bytes 52
  0.8 16.6 %collective-permute-start.3 = (bf16[2,2,256,128]{3,2,1,0:T(8,128)(2,1)}, bf16[2,2,256,128]{3,2,1,0:T(8,128)(2,1)S(1)}, u32[]{:S(2)}, u32[]{:S(2)}) collective-permute-start(bf16[2,2,256,128]{3,2,1,0:T(8,128)(2,1)} %refs_0_.1), channel_id=1, source_target_pairs={{0,8},{12,4},{4,0},{8,12},{1,9},{13,5},{5,1},{9,13},{2,10},{14,6},... | collective-permute-start | bytes 786440 | tf_op jit(solution)/shard_map/ppermute | solution.py:475
  4.8 13.3 %collective-permute-start.4 = (bf16[2,2,256,128]{3,2,1,0:T(8,128)(2,1)}, bf16[2,2,256,128]{3,2,1,0:T(8,128)(2,1)S(1)}, u32[]{:S(2)}, u32[]{:S(2)}) collective-permute-start(bf16[2,2,256,128]{3,2,1,0:T(8,128)(2,1)} %refs_0_.1), channel_id=1, source_target_pairs={{4,12},{8,0},{0,4},{12,8},{5,13},{9,1},{1,5},{13,9},{6,14},{10,2},... | collective-permute-start | bytes 786440 | tf_op jit(solution)/shard_map/ppermute | solution.py:475
  7.6 4.3 %collective-permute-start = (bf16[96,256]{1,0:T(8,128)(2,1)}, bf16[96,256]{1,0:T(8,128)(2,1)S(1)}, u32[]{:S(2)}, u32[]{:S(2)}) collective-permute-start(bf16[96,256]{1,0:T(8,128)(2,1)} %get-tuple-element.13), channel_id=1, source_target_pairs={{0,3},{1,2},{2,1},{3,0},{4,7},{5,6},{6,5},{7,4},{8,11},{9,10},{10,... | collective-permute-start | bytes 147464 | tf_op jit(solution)/shard_map/ppermute | solution.py:483
  8.4 4.8 %collective-permute-start.1 = (bf16[96,256]{1,0:T(8,128)(2,1)}, bf16[96,256]{1,0:T(8,128)(2,1)S(1)}, u32[]{:S(2)}, u32[]{:S(2)}) collective-permute-start(bf16[96,256]{1,0:T(8,128)(2,1)} %get-tuple-element.14), channel_id=1, source_target_pairs={{0,2},{1,3},{2,0},{3,1},{4,6},{5,7},{6,4},{7,5},{8,10},{9,11},{10,... | collective-permute-start | bytes 147464 | tf_op jit(solution)/shard_map/ppermute | solution.py:483
  9.3 3.9 %collective-permute-start.2 = (bf16[96,256]{1,0:T(8,128)(2,1)}, bf16[96,256]{1,0:T(8,128)(2,1)S(1)}, u32[]{:S(2)}, u32[]{:S(2)}) collective-permute-start(bf16[96,256]{1,0:T(8,128)(2,1)} %get-tuple-element.15), channel_id=1, source_target_pairs={{0,1},{1,0},{2,3},{3,2},{4,5},{5,4},{6,7},{7,6},{8,9},{9,8},{10,11... | collective-permute-start | bytes 147464 | tf_op jit(solution)/shard_map/ppermute | solution.py:483
  9.9 0.8 %copy-start.2 = (bf16[96,256]{1,0:T(8,128)(2,1)S(1)}, bf16[96,256]{1,0:T(8,128)(2,1)}, u32[]{:S(2)}) copy-start(bf16[96,256]{1,0:T(8,128)(2,1)} %get-tuple-element.12.value_ref) | copy-start | bytes 147460
  13.9 6.0 %collective-permute-start.6 = (bf16[2,2,48,128]{3,2,1,0:T(8,128)(2,1)S(1)}, bf16[2,2,48,128]{3,2,1,0:T(8,128)(2,1)S(1)}, u32[]{:S(2)}, u32[]{:S(2)}) collective-permute-start(bf16[2,2,48,128]{3,2,1,0:T(8,128)(2,1)S(1)} %get-tuple-element.17.ahead_ref.refs_3_), channel_id=1, source_target_pairs={{0,8},{4,12},{8,0},{12,4},{1,9},{5,13},{9,1},{13,5},{2,10},{6,14},... | collective-permute-start | bytes 147464 | tf_op jit(solution)/shard_map/ppermute | solution.py:470
  16.5 4.4 %collective-permute-start.8 = (bf16[2,2,48,128]{3,2,1,0:T(8,128)(2,1)S(1)}, bf16[2,2,48,128]{3,2,1,0:T(8,128)(2,1)S(1)}, u32[]{:S(2)}, u32[]{:S(2)}) collective-permute-start(bf16[2,2,48,128]{3,2,1,0:T(8,128)(2,1)S(1)} %get-tuple-element.17.ahead_ref.refs_3_), channel_id=1, source_target_pairs={{0,4},{4,0},{8,12},{12,8},{1,5},{5,1},{9,13},{13,9},{2,6},{6,2},{1... | collective-permute-start | bytes 147464 | tf_op jit(solution)/shard_map/ppermute | solution.py:470
  18.2 9.3 %collective-permute-start.5 = (bf16[2,2,256,128]{3,2,1,0:T(8,128)(2,1)S(1)}, bf16[2,2,256,128]{3,2,1,0:T(8,128)(2,1)S(1)}, u32[]{:S(2)}, u32[]{:S(2)}) collective-permute-start(bf16[2,2,256,128]{3,2,1,0:T(8,128)(2,1)S(1)} %assemble.1.refs_0_), channel_id=1, source_target_pairs={{0,4},{4,0},{8,12},{12,8},{1,5},{5,1},{9,13},{13,9},{2,6},{6,2},{1... | collective-permute-start | bytes 786440 | tf_op jit(solution)/shard_map/ppermute | solution.py:470
  19.9 7.5 %collective-permute-start.7 = (bf16[2,2,48,128]{3,2,1,0:T(8,128)(2,1)S(1)}, bf16[2,2,48,128]{3,2,1,0:T(8,128)(2,1)S(1)}, u32[]{:S(2)}, u32[]{:S(2)}) collective-permute-start(bf16[2,2,48,128]{3,2,1,0:T(8,128)(2,1)S(1)} %hold.3), channel_id=1, source_target_pairs={{0,4},{4,0},{8,12},{12,8},{1,5},{5,1},{9,13},{13,9},{2,6},{6,2},{1... | collective-permute-start | bytes 147464 | tf_op jit(solution)/shard_map/ppermute | solution.py:470

commit v4 on v3

--- a/solution.py
+++ b/solution.py
@@ -52,24 +52,24 @@
     return [jnp.where(slots[0] >= 0, slots[0], slots[1]), jnp.where(slots[0] >= 0, slots[1], -1)]
 
 
-def project_body(me_ref, hidden_ref, gain_ref, weight_ref, *refs):
-    *pieces, held, gain, weights, whole, sems = refs
-    chunks, depth, width = weights.shape
+def project_body(ks, me_ref, hidden_ref, gain_ref, weight_ref, *refs):
+    *pieces, held, gain, weights, sems = refs
     slots, rows, features = held.shape
     count = slots * rows
     height, columns = pieces[0].shape
     spare = height - count
 
-    def chunk(k):
-        part = weight_ref.at[pl.ds(k * depth, depth)]
-        return pltpu.make_async_copy(part, weights.at[k], sems.at[2 + k])
+    def block(at, k):
+        first = pl.multiple_of((me_ref[0] ^ k) * columns, columns)
+        part = weight_ref.at[:, pl.ds(first, columns)]
+        return pltpu.make_async_copy(part, weights.at[at], sems.at[2 + at])
 
     arrive = pltpu.make_async_copy(hidden_ref, held, sems.at[0])
     follow = pltpu.make_async_copy(gain_ref, gain, sems.at[1])
     arrive.start()
     follow.start()
-    for k in range(chunks):
-        chunk(k).start()
+    for at, k in enumerate(ks):
+        block(at, k).start()
     arrive.wait()
     follow.wait()
     hidden = held[...].astype(jnp.float32).reshape(count, features)
@@ -88,34 +88,27 @@
     both = jnp.where(row == 0, coarse, jnp.where(row == 1, total - coarse, 0.0))
     rest = jnp.zeros((spare, columns - total.shape[1]), jnp.float32)
     tail = jnp.concatenate([both, rest], 1).astype(jnp.bfloat16)
-    product = jnp.zeros((count, width), jnp.float32)
-    for k in range(chunks):
-        chunk(k).wait()
-        part = scaled[:, k * depth : (k + 1) * depth]
-        product += jnp.dot(part, weights[k], preferred_element_type=jnp.float32)
-    whole[...] = product
-    for k, piece in enumerate(pieces):
-        at = pl.multiple_of((me_ref[0] ^ k) * columns, columns)
-        piece[:count] = whole[:, pl.ds(at, columns)].astype(jnp.bfloat16)
-        piece[count:] = tail
-
-
-def project(me, hidden_rows, norm_gain, kv_weight, parts):
+    for at, k in enumerate(ks):
+        block(at, k).wait()
+        product = jnp.dot(scaled, weights[at], preferred_element_type=jnp.float32)
+        pieces[at][:count] = product.astype(jnp.bfloat16)
+        pieces[at][count:] = tail
+
+
+def project(me, hidden_rows, norm_gain, kv_weight, parts, ks):
     slots, rows, features = hidden_rows.shape
     columns = kv_weight.shape[1] // parts
-    chunks = 4
     shape = (slots * rows + 16, columns)
     return pl.pallas_call(
-        project_body,
-        out_shape=[jax.ShapeDtypeStruct(shape, jnp.bfloat16)] * parts,
+        functools.partial(project_body, ks),
+        out_shape=[jax.ShapeDtypeStruct(shape, jnp.bfloat16)] * len(ks),
         in_specs=[pl.BlockSpec(memory_space=SMEM)] + [pl.BlockSpec(memory_space=pltpu.HBM)] * 3,
-        out_specs=[pl.BlockSpec(memory_space=VMEM)] * parts,
+        out_specs=[pl.BlockSpec(memory_space=VMEM)] * len(ks),
         scratch_shapes=[
             pltpu.VMEM(hidden_rows.shape, jnp.bfloat16),
             pltpu.VMEM(norm_gain.shape, jnp.bfloat16),
-            pltpu.VMEM((chunks, features // chunks, kv_weight.shape[1]), jnp.bfloat16),
-            pltpu.VMEM((slots * rows, kv_weight.shape[1]), jnp.float32),
-            pltpu.SemaphoreType.DMA((2 + chunks,)),
+            pltpu.VMEM((len(ks), features, columns), jnp.bfloat16),
+            pltpu.SemaphoreType.DMA((2 + len(ks),)),
         ],
         cost_estimate=pl.CostEstimate(flops=1000, bytes_accessed=1000, transcendentals=0),
         compiler_params=pltpu.CompilerParams(vmem_limit_bytes=PROJECT_VMEM),
@@ -123,9 +116,9 @@
     )(me, hidden_rows, norm_gain, kv_weight)
 
 
-def finish_body(features, marks_ref, *refs):
-    pieces, (fresh_ref, payload_ref) = refs[:-2], refs[-2:]
-    slots, _, rows, width = fresh_ref.shape
+def finish_body(features, rows, marks_ref, *refs):
+    *pieces, payload_ref = refs
+    slots, _, padded, width = payload_ref.shape
     count = slots * rows
     total = pieces[0][...].astype(jnp.float32)
     for piece in pieces[1:]:
@@ -138,19 +131,16 @@
         values = total[:count, half * width : (half + 1) * width] * inverse
         for slot in range(slots):
             mine = values[slot * rows : (slot + 1) * rows]
-            fresh_ref[slot, half] = mine.astype(jnp.bfloat16)
-            marks = jnp.broadcast_to(marks_ref[slot : slot + 1], (payload_ref.shape[2] - rows, width))
+            marks = jnp.broadcast_to(marks_ref[slot : slot + 1], (padded - rows, width))
             marked = jnp.concatenate([mine, marks], 0)
             payload_ref[slot, half] = marked.astype(jnp.bfloat16)
 
 
 def finish(pieces, marks, slots, rows, width, features):
+    shape = (slots, 2, round_up(rows + 1, 16), width)
     return pl.pallas_call(
-        functools.partial(finish_body, features),
-        out_shape=[
-            jax.ShapeDtypeStruct((slots, 2, rows, width), jnp.bfloat16),
-            jax.ShapeDtypeStruct((slots, 2, round_up(rows + 1, 16), width), jnp.bfloat16),
-        ],
+        functools.partial(finish_body, features, rows),
+        out_shape=jax.ShapeDtypeStruct(shape, jnp.bfloat16),
         cost_estimate=pl.CostEstimate(flops=1000, bytes_accessed=1000, transcendentals=0),
         compiler_params=pltpu.CompilerParams(vmem_limit_bytes=8 << 20),
         name="finish",
@@ -255,13 +245,28 @@
 
 def early_body(pieces, locate, rows, factor, slot_ref, length_ref, place_ref, seq_ref, *refs):
     cached, fresh, refs = refs[:pieces], refs[pieces : 2 * pieces], refs[2 * pieces :]
-    query_ref, query_at_ref, query_cos_ref, query_sin_ref, *tables = refs[:8]
-    turned, top, mass, total, cached_buf, fresh_buf, keys_buf, values_buf, sems = refs[8:]
+    payload_ref, query_ref, query_at_ref, query_cos_ref, query_sin_ref, *tables = refs[:9]
+    turned, top, mass, total, facts, mine_ref, cached_buf, fresh_buf, keys_buf, values_buf, sems = refs[9:]
     slots, _, columns = query_ref.shape
     span, width = cached_buf.shape[-2:]
     group = columns // width
     stretches = slot_ref.shape[0]
     last = functools.reduce(jnp.maximum, [place_ref[s] for s in range(slots)])
+    for slot in range(slots):
+        for half in range(2):
+            mine_ref[slot, half] = payload_ref[slot, half].astype(jnp.float32)[:rows].astype(jnp.bfloat16)
+    chosen = far_slots(seq_ref[0], slot_ref) if pieces > 1 else []
+    known = []
+    for slot in chosen:
+        place = place_of(slot, slot_ref)
+        end = jnp.where(place >= 0, length_ref[jnp.maximum(place, 0)], 0)
+        known += [jnp.where(slot >= 0, slot % 2, -1), place, end]
+    known = [place_ref[slot] for slot in range(slots)] + known
+    lane = lax.broadcasted_iota(jnp.int32, facts.shape, 1)
+    line = jnp.zeros(facts.shape, jnp.int32)
+    for k, value in enumerate(known):
+        line = jnp.where(lane == k, value, line)
+    facts[...] = line
 
     def there(position):
         places = locate(slot_ref[position], seq_ref[0], slot_ref)
@@ -362,51 +367,51 @@
     lax.fori_loop(0, last + 1, stretch, 0)
 
 
-def late_body(exchanged, rows, factor, slot_ref, length_ref, place_ref, seq_ref, *refs):
+def late_body(exchanged, rows, factor, *refs):
     if exchanged:
         message, fresh, *tables = refs[:6]
         refs = refs[6:]
-    query_at_ref, turned, early_top, early_mass, early_total, out_ref, keys_buf, values_buf = refs
-    slots, _, columns = out_ref.shape
+    turned, early_top, early_mass, early_total, facts, out_ref, *refs = refs
+    out_buf, keys_buf, values_buf, sems = refs
+    slots, _, columns = out_buf.shape
     width = turned.shape[-1]
     group = columns // width
+    mine = [facts[0, slot] for slot in range(slots)]
 
     def write(slot, result):
         for head in range(group):
-            mine = result[head * rows : (head + 1) * rows]
-            out_ref[slot, :, head * width : (head + 1) * width] = mine.astype(jnp.bfloat16)
-
-    def plain(slot):
-        write(slot, early_total[slot] / early_mass[slot])
-
+            part = result[head * rows : (head + 1) * rows]
+            out_buf[slot, :, head * width : (head + 1) * width] = part.astype(jnp.bfloat16)
+
+    def leave(slot):
+        return pltpu.make_async_copy(out_buf.at[slot], out_ref.at[slot], sems.at[slot])
+
+    chosen = [[facts[0, slots + 3 * k + j] for j in range(3)] for k in range(2)] if exchanged else []
+    touched = [
+        functools.reduce(
+            jnp.logical_or, [(at >= 0) & (place < mine[slot]) for at, place, _ in chosen], jnp.bool_(False)
+        )
+        for slot in range(slots)
+    ]
     for slot in range(slots):
 
-        @pl.when(place_ref[slot] < 0)
+        @pl.when(mine[slot] < 0)
         def _(slot=slot):
-            out_ref[slot] = jnp.zeros_like(out_ref[slot])
-
-    if not exchanged:
-        for slot in range(slots):
-            pl.when(place_ref[slot] >= 0)(functools.partial(plain, slot))
-        return
-
-    _, _, span, _ = message.shape
-    seq = seq_ref[0]
-    chosen = far_slots(seq, slot_ref)
-    places = [place_of(slot, slot_ref) for slot in chosen]
-    for k, slot in enumerate(chosen):
-        @pl.when(slot >= 0)
-        def _(k=k, slot=slot):
-            keys_buf[k], values_buf[k] = ready(
-                message.at[slot % 2], fresh.at[slot % 2], places[k], rows, tables
-            )
-
-    index = lax.broadcasted_iota(jnp.int32, (1, span), 1)
+            out_buf[slot] = jnp.zeros_like(out_buf[slot])
+            leave(slot).start()
+
+        @pl.when((mine[slot] >= 0) & jnp.logical_not(touched[slot]))
+        def _(slot=slot):
+            write(slot, early_total[slot] / early_mass[slot])
+            leave(slot).start()
 
     def settle(slot, count):
+        span = message.shape[2]
+        index = lax.broadcasted_iota(jnp.int32, (1, span), 1)
         scores = []
         for k in range(count):
-            end = jnp.where(places[k] < place_ref[slot], length_ref[places[k]], 0)
+            _, place, length = chosen[k]
+            end = jnp.where(place < mine[slot], length, 0)
             scores.append(score(turned[slot], keys_buf[k]) + jnp.where(index < end, 0.0, FAR))
         scores = jnp.concatenate(scores, 1)
         before = early_top[slot]
@@ -418,13 +423,25 @@
         added = jnp.dot(weight.astype(jnp.bfloat16), values, preferred_element_type=jnp.float32)
         write(slot, (early_total[slot] * fade + added) / mass)
 
-    count = jnp.where(chosen[1] >= 0, 2, jnp.where(chosen[0] >= 0, 1, 0))
+    def take(count):
+        for k in range(count):
+            at, place, _ = chosen[k]
+            keys_buf[k], values_buf[k] = ready(message.at[at], fresh.at[at], place, rows, tables)
+        for slot in range(slots):
+
+            @pl.when(touched[slot])
+            def _(slot=slot):
+                settle(slot, count)
+                leave(slot).start()
+
+    if exchanged:
+        pl.when((chosen[0][0] >= 0) & (chosen[1][0] < 0))(functools.partial(take, 1))
+        pl.when(chosen[1][0] >= 0)(functools.partial(take, 2))
     for slot in range(slots):
-        for cases, act in ((0, plain), (1, functools.partial(settle, count=1)), (2, functools.partial(settle, count=2))):
-            pl.when((place_ref[slot] >= 0) & (count == cases))(functools.partial(act, slot))
-
-
-def attend(body, lists, far, near, out_shape, scratch, cost):
+        leave(slot).wait()
+
+
+def attend(body, lists, far, near, out_shape, out_space, scratch, cost):
     specs = [pl.BlockSpec(memory_space=SMEM)] * len(lists)
     specs += [pl.BlockSpec(memory_space=pl.ANY)] * len(far)
     specs += [pl.BlockSpec(memory_space=VMEM)] * len(near)
@@ -432,7 +449,7 @@
         body,
         out_shape=out_shape,
         in_specs=specs,
-        out_specs=jax.tree.map(lambda _: pl.BlockSpec(memory_space=VMEM), out_shape),
+        out_specs=jax.tree.map(lambda _: pl.BlockSpec(memory_space=out_space), out_shape),
         scratch_shapes=scratch,
         cost_estimate=pl.CostEstimate(flops=cost, bytes_accessed=1000, transcendentals=0),
         compiler_params=pltpu.CompilerParams(vmem_limit_bytes=32 << 20),
@@ -476,12 +493,18 @@
 
     marks = jnp.pad(recompute_rows.astype(jnp.float32), ((0, 0), (0, width - rows)), constant_values=-1.0)
 
-    pieces = project(me.reshape(1), hidden_rows, norm_gain, kv_weight, parts)
-    sums = [hold(pieces[0])]
-    for distance in range(parts - 1, 0, -1):
-        swap = [(i, i ^ distance) for i in range(parts)]
-        sums.append(lax.ppermute(pieces[distance], FEATURES, swap))
-    fresh_kv, payload = finish(sums, marks, slots, rows, width, features)
+    def part(ks):
+        return project(me.reshape(1), hidden_rows, norm_gain, kv_weight, parts, ks)
+
+    def hand(piece, distance):
+        return lax.ppermute(piece, FEATURES, [(i, i ^ distance) for i in range(parts)])
+
+    away = tuple(range(parts - 1, 1, -1))
+    sums = [hand(piece, distance) for piece, distance in zip(part(away), away)]
+    near, own = part((1, 0))
+    sums += [hand(near, 1), hold(own)]
+
+    payload = finish(sums, marks, slots, rows, width, features)
 
     mine = seq * slots + jnp.arange(slots, dtype=jnp.int32)
     hits = stretch_slot[:, None] == mine[None]
@@ -513,12 +536,16 @@
     factor = width ** (-0.5) * math.log2(math.e)
     state = (slots, lines, width)
     stage = pltpu.VMEM(((stretches if stretches <= 4 else 1) * span, width), jnp.bfloat16)
-    passed = attend(
+    *passed, fresh_kv = attend(
         functools.partial(early_body, len(early[0]), locate, rows, factor),
         lists,
         (*early[0], *early[1]),
-        (queries, *query_tables, *tables),
-        [jax.ShapeDtypeStruct(state, jnp.bfloat16)] + [jax.ShapeDtypeStruct(state, jnp.float32)] * 3,
+        (payload, queries, *query_tables, *tables),
+        [jax.ShapeDtypeStruct(state, jnp.bfloat16)]
+        + [jax.ShapeDtypeStruct(state, jnp.float32)] * 3
+        + [jax.ShapeDtypeStruct((8, 128), jnp.int32)]
+        + [jax.ShapeDtypeStruct((slots, 2, rows, width), jnp.bfloat16)],
+        VMEM,
         [
             pltpu.VMEM((stretches, 2, span, width), jnp.bfloat16),
             pltpu.VMEM((stretches, 2, padded, width), jnp.bfloat16),
@@ -530,13 +557,16 @@
     )
     attended = attend(
         functools.partial(late_body, exchanged, rows, factor),
-        lists,
         (),
-        (*late, query_tables[0], *passed),
+        (),
+        (*late, *passed),
         jax.ShapeDtypeStruct(queries.shape, jnp.bfloat16),
+        pl.ANY,
         [
+            pltpu.VMEM(queries.shape, jnp.bfloat16),
             pltpu.VMEM((2, span, width), jnp.bfloat16),
             pltpu.VMEM((2, span, width), jnp.bfloat16),
+            pltpu.SemaphoreType.DMA((slots,)),
         ],
         1000,
     )

time: 29.9 us -> 29.2 us (0.977)
  waiting for transfers between devices: 7.66 us -> 5.89 us
  Pallas kernels: 9.08 us -> 10 us
    ppermute x3, waiting for transfers between devices: 2.51 us -> 0.04 us  [hand(): lax.ppermute(piece, FEATURES, [(i, i ^ distance) for i in range(parts)])]
    pallas_call x2 -> x3, Pallas kernels: 3.51 us -> 5.01 us  [the longest x2 4.91 us: project(): pl.pallas_call(functools.partial(project_body, ks), out_shape=[jax.ShapeD...]
    pallas_call x2, Pallas kernels: 5.53 us -> 4.98 us  [attend(): pl.pallas_call(body, out_shape=out_shape, in_specs=specs, out_specs=jax.t...]
    ppermute x2, waiting for transfers between devices: 0.73 us -> 1.09 us  [local(): lax.ppermute(pool_kv, 'seq', pairs)]
    ppermute x4, waiting for transfers between devices: 4.42 us -> 4.76 us  [along_seq(): lax.ppermute(value, 'seq', [(z, z ^ distance) for z in range(seq_count)])]
  transfers between devices with their start and end apart: 9 -> 9, of which waited for: 5 -> 3; matrix products, arithmetic and copies ran while one was open for 2% -> 2% of each run, Pallas kernels for 22% -> 29%
where the time goes in v4:
time: 29.2 us; the launch traced here: 28.9 us
  starting transfers between devices  10.7 us (37%)
  Pallas kernels  10 us (34%)
  waiting for transfers between devices  5.89 us (20%)
  local copies, waits for them, and re-layouts  0.94 us (3%)
  between operations  0.84 us (3%)
  other arithmetic  0.49 us (2%)
    pallas_call x2, Pallas kernels, attend(): pl.pallas_call(body, out_shape=out_shape, in_specs=specs, out_specs=jax.t...  4.98 us
    pallas_call x2, Pallas kernels, project(): pl.pallas_call(functools.partial(project_body, ks), out_shape=[jax.ShapeD...  4.91 us
    ppermute x4, waiting for transfers between devices, along_seq(): lax.ppermute(value, 'seq', [(z, z ^ distance) for z in range(seq_count)])  4.76 us
    ppermute x4, starting transfers between devices, along_seq(): lax.ppermute(value, 'seq', [(z, z ^ distance) for z in range(seq_count)])  4.66 us
    ppermute x2, starting transfers between devices, local(): lax.ppermute(pool_kv, 'seq', pairs)  4.09 us
    ppermute x3, starting transfers between devices, hand(): lax.ppermute(piece, FEATURES, [(i, i ^ distance) for i in range(parts)])  1.99 us
    ppermute x2, waiting for transfers between devices, local(): lax.ppermute(pool_kv, 'seq', pairs)  1.09 us
    unnamed x24, local copies, waits for them, and re-layouts  0.86 us
  transfers between devices with their start and end apart: 9, of which 3 were waited for; matrix products, arithmetic and copies ran while one was open for 2% of the time, Pallas kernels for 29%

profile of v4, /device:TPU:0, one launch (start us, length us, event | category | flops | bytes accessed | tf_op | source)
XLA Modules:
  0.0 28.9 jit_solution(5629383435895593938)
XLA Ops:
  0.6 4.1 %collective-permute-start = (bf16[2,2,256,128]{3,2,1,0:T(8,128)(2,1)}, bf16[2,2,256,128]{3,2,1,0:T(8,128)(2,1)S(1)}, u32[]{:S(2)}, u32[]{:S(2)}) collective-permute-start(bf16[2,2,256,128]{3,2,1,0:T(8,128)(2,1)} %refs_0_.1), channel_id=1, source_target_pairs={{0,8},{12,4},{4,0},{8,12},{1,9},{13,5},{5,1},{9,13},{2,10},{14,6},... | collective-permute-start | bytes 786440 | tf_op jit(solution)/shard_map/ppermute | solution.py:492
  4.7 0.0 copy-start.11
  4.7 2.5 %project.2 = (bf16[96,256]{1,0:T(8,128)(2,1)}, bf16[96,256]{1,0:T(8,128)(2,1)}) custom-call(s32[1]{0:T(128)} %bitcast.1.me_ref, bf16[2,40,1024]{2,1,0:T(8,128)(2,1)} %hidden_ref.3, bf16[1024]{0:T(1024)(128)(2,1)} %gain_ref.3, bf16[1024,1024]{1,0:T(8,128)(2,1)} %weight_ref.3), custom_call_target="tpu_custom_call" | custom-call | flops 1000 | bytes 1000 | tf_op jit(solution)/shard_map/project/pallas_call | solution.py:102
  7.3 0.7 %collective-permute-start.2 = (bf16[96,256]{1,0:T(8,128)(2,1)}, bf16[96,256]{1,0:T(8,128)(2,1)S(1)}, u32[]{:S(2)}, u32[]{:S(2)}) collective-permute-start(bf16[96,256]{1,0:T(8,128)(2,1)} %get-tuple-element.12), channel_id=1, source_target_pairs={{0,3},{1,2},{2,1},{3,0},{4,7},{5,6},{6,5},{7,4},{8,11},{9,10},{10,... | collective-permute-start | bytes 147464 | tf_op jit(solution)/shard_map/ppermute | solution.py:500
  8.0 0.9 %collective-permute-start.3 = (bf16[96,256]{1,0:T(8,128)(2,1)}, bf16[96,256]{1,0:T(8,128)(2,1)S(1)}, u32[]{:S(2)}, u32[]{:S(2)}) collective-permute-start(bf16[96,256]{1,0:T(8,128)(2,1)} %get-tuple-element.13), channel_id=1, source_target_pairs={{0,2},{1,3},{2,0},{3,1},{4,6},{5,7},{6,4},{7,5},{8,10},{9,11},{10,... | collective-permute-start | bytes 147464 | tf_op jit(solution)/shard_map/ppermute | solution.py:500
  9.0 2.4 %project.3 = (bf16[96,256]{1,0:T(8,128)(2,1)}, bf16[96,256]{1,0:T(8,128)(2,1)}) custom-call(s32[1]{0:T(128)} %bitcast.1.me_ref, bf16[2,40,1024]{2,1,0:T(8,128)(2,1)} %hidden_ref.3, bf16[1024]{0:T(1024)(128)(2,1)} %gain_ref.3, bf16[1024,1024]{1,0:T(8,128)(2,1)} %weight_ref.3), custom_call_target="tpu_custom_call" | custom-call | flops 1000 | bytes 1000 | tf_op jit(solution)/shard_map/project/pallas_call | solution.py:102
  11.4 0.4 %collective-permute-start.4 = (bf16[96,256]{1,0:T(8,128)(2,1)}, bf16[96,256]{1,0:T(8,128)(2,1)S(1)}, u32[]{:S(2)}, u32[]{:S(2)}) collective-permute-start(bf16[96,256]{1,0:T(8,128)(2,1)} %get-tuple-element.14), channel_id=1, source_target_pairs={{0,1},{1,0},{2,3},{3,2},{4,5},{5,4},{6,7},{7,6},{8,9},{9,8},{10,11... | collective-permute-start | bytes 147464 | tf_op jit(solution)/shard_map/ppermute | solution.py:500
  11.8 0.2 fusion.1.place_ref
  12.0 0.1 fusion.2
  12.0 0.8 %copy-done.2 = bf16[96,256]{1,0:T(8,128)(2,1)S(1)} copy-done((bf16[96,256]{1,0:T(8,128)(2,1)S(1)}, bf16[96,256]{1,0:T(8,128)(2,1)}, u32[]{:S(2)}) %copy-start.2) | copy-done | bytes 49176
  12.9 0.0 collective-permute-done.4.refs_2_
  12.9 0.1 finish.1.refs_3_.refs_6_.ahead_ref
  13.0 3.0 %collective-permute-start.6 = (bf16[2,2,48,128]{3,2,1,0:T(8,128)(2,1)S(1)}, bf16[2,2,48,128]{3,2,1,0:T(8,128)(2,1)S(1)}, u32[]{:S(2)}, u32[]{:S(2)}) collective-permute-start(bf16[2,2,48,128]{3,2,1,0:T(8,128)(2,1)S(1)} %finish.1.refs_3_.refs_6_.ahead_ref), channel_id=1, source_target_pairs={{0,8},{4,12},{8,0},{12,4},{1,9},{5,13},{9,1},{13,5},{2,10},{6,14},... | collective-permute-start | bytes 147464 | tf_op jit(solution)/shard_map/ppermute | solution.py:487
  16.0 0.7 %collective-permute-start.5 = (bf16[2,2,48,128]{3,2,1,0:T(8,128)(2,1)S(1)}, bf16[2,2,48,128]{3,2,1,0:T(8,128)(2,1)S(1)}, u32[]{:S(2)}, u32[]{:S(2)}) collective-permute-start(bf16[2,2,48,128]{3,2,1,0:T(8,128)(2,1)S(1)} %finish.1.refs_3_.refs_6_.ahead_ref), channel_id=1, source_target_pairs={{0,4},{4,0},{8,12},{12,8},{1,5},{5,1},{9,13},{13,9},{2,6},{6,2},{1... | collective-permute-start | bytes 147464 | tf_op jit(solution)/shard_map/ppermute | solution.py:487
  16.7 0.2 fusion
  16.9 1.1 %collective-permute-done.1.refs_2_.two_ref = bf16[2,2,256,128]{3,2,1,0:T(8,128)(2,1)S(1)} collective-permute-done((bf16[2,2,256,128]{3,2,1,0:T(8,128)(2,1)}, bf16[2,2,256,128]{3,2,1,0:T(8,128)(2,1)S(1)}, u32[]{:S(2)}, u32[]{:S(2)}) %collective-permute-start.1) | collective-permute-done | bytes 262176 | tf_op jit(solution)/shard_map/ppermute | solution.py:492
  18.0 0.7 %collective-permute-start.7 = (bf16[2,2,256,128]{3,2,1,0:T(8,128)(2,1)S(1)}, bf16[2,2,256,128]{3,2,1,0:T(8,128)(2,1)S(1)}, u32[]{:S(2)}, u32[]{:S(2)}) collective-permute-start(bf16[2,2,256,128]{3,2,1,0:T(8,128)(2,1)S(1)} %assemble.1.refs_0_), channel_id=1, source_target_pairs={{0,4},{4,0},{8,12},{12,8},{1,5},{5,1},{9,13},{13,9},{2,6},{6,2},{1... | collective-permute-start | bytes 786440 | tf_op jit(solution)/shard_map/ppermute | solution.py:487
  18.7 1.3 %collective-permute-done.6.refs_5_.value_ref = bf16[2,2,48,128]{3,2,1,0:T(8,128)(2,1)S(1)} collective-permute-done((bf16[2,2,48,128]{3,2,1,0:T(8,128)(2,1)S(1)}, bf16[2,2,48,128]{3,2,1,0:T(8,128)(2,1)S(1)}, u32[]{:S(2)}, u32[]{:S(2)}) %collective-permute-start.6) | collective-permute-done | bytes 49184 | tf_op jit(solution)/shard_map/ppermute | solution.py:487
  20.0 0.3 %collective-permute-start.8 = (bf16[2,2,48,128]{3,2,1,0:T(8,128)(2,1)S(1)}, bf16[2,2,48,128]{3,2,1,0:T(8,128)(2,1)S(1)}, u32[]{:S(2)}, u32[]{:S(2)}) collective-permute-start(bf16[2,2,48,128]{3,2,1,0:T(8,128)(2,1)S(1)} %hold.3), channel_id=1, source_target_pairs={{0,4},{4,0},{8,12},{12,8},{1,5},{5,1},{9,13},{13,9},{2,6},{6,2},{1... | collective-permute-start | bytes 147464 | tf_op jit(solution)/shard_map/ppermute | solution.py:487
  20.4 0.0 collective-permute-done.5.refs_4_
  20.4 0.1 broadcast_in_dim.16.refs_8_
  20.5 3.4 %early_body.1 = (bf16[2,320,128]{2,1,0:T(8,128)(2,1)S(1)}, f32[2,320,128]{2,1,0:T(8,128)S(1)}, f32[2,320,128]{2,1,0:T(8,128)S(1)}, f32[2,320,128]{2,1,0:T(8,128)...) custom-call(s32[4]{0:T(128)S(1)} %copy-done.7, s32[4]{0:T(128)S(1)} %copy-done.8, s32[2]{0:T(128)S(1)} %fusion.1.place_ref, ...), custom_call_target="tpu_custom_call" | custom-call | flops 3000000000 | bytes 1000 | tf_op jit(solution)/shard_map/early_body/pallas_call | solution.py:448
  23.9 3.4 %collective-permute-done.8.refs_1_ = bf16[2,2,48,128]{3,2,1,0:T(8,128)(2,1)S(1)} collective-permute-done((bf16[2,2,48,128]{3,2,1,0:T(8,128)(2,1)S(1)}, bf16[2,2,48,128]{3,2,1,0:T(8,128)(2,1)S(1)}, u32[]{:S(2)}, u32[]{:S(2)}) %collective-permute-start.8) | collective-permute-done | bytes 49184 | tf_op jit(solution)/shard_map/ppermute | solution.py:487
  27.3 1.6 %late_body.1 = bf16[2,40,1024]{2,1,0:T(8,128)(2,1)} custom-call(bf16[2,2,256,128]{3,2,1,0:T(8,128)(2,1)S(1)} %collective-permute-done.7.refs_0_, bf16[2,2,48,128]{3,2,1,0:T(8,128)(2,1)S(1)} %collective-permute-done.8.refs_1_, f32[256,128]{1,0:T(8,128)S(1)} %copy-done, f32[256,128]{1,0:T(8,128)S(1)} %copy-done.1, f32[4,128]{1,0:T(4,128)S(1)} %copy-done.3, ...), custom_call_target="tpu_custom_call" | custom-call | flops 1000 | bytes 1000 | tf_op jit(solution)/shard_map/late_body/pallas_call | solution.py:448
  (33 shorter events, 0.1 us)
Async XLA Ops:
  0.6 16.3 %collective-permute-start = (bf16[2,2,256,128]{3,2,1,0:T(8,128)(2,1)}, bf16[2,2,256,128]{3,2,1,0:T(8,128)(2,1)S(1)}, u32[]{:S(2)}, u32[]{:S(2)}) collective-permute-start(bf16[2,2,256,128]{3,2,1,0:T(8,128)(2,1)} %refs_0_.1), channel_id=1, source_target_pairs={{0,8},{12,4},{4,0},{8,12},{1,9},{13,5},{5,1},{9,13},{2,10},{14,6},... | collective-permute-start | bytes 786440 | tf_op jit(solution)/shard_map/ppermute | solution.py:492
  4.7 13.3 %collective-permute-start.1 = (bf16[2,2,256,128]{3,2,1,0:T(8,128)(2,1)}, bf16[2,2,256,128]{3,2,1,0:T(8,128)(2,1)S(1)}, u32[]{:S(2)}, u32[]{:S(2)}) collective-permute-start(bf16[2,2,256,128]{3,2,1,0:T(8,128)(2,1)} %refs_0_.1), channel_id=1, source_target_pairs={{4,12},{8,0},{0,4},{12,8},{5,13},{9,1},{1,5},{13,9},{6,14},{10,2},... | collective-permute-start | bytes 786440 | tf_op jit(solution)/shard_map/ppermute | solution.py:492
  4.7 7.0 %copy-start.7 = (s32[4]{0:T(128)S(1)}, s32[4]{0:T(128)}, u32[]{:S(2)}) copy-start(s32[4]{0:T(128)} %slot_ref.1) | copy-start | bytes 52
  4.7 7.2 %copy-start.9 = (s32[2,40]{1,0:T(2,128)S(1)}, s32[2,40]{1,0:T(2,128)}, u32[]{:S(2)}) copy-start(s32[2,40]{1,0:T(2,128)} %param.21) | copy-start | bytes 964
  4.7 11.9 %copy-start.10 = (f32[128]{0:T(128)S(1)}, f32[128]{0:T(128)}, u32[]{:S(2)}) copy-start(f32[128]{0:T(128)} %constant.33.clone) | copy-start | bytes 1540
  4.7 11.9 %copy-start.11 = (f32[128]{0:T(128)S(1)}, f32[128]{0:T(128)}, u32[]{:S(2)}) copy-start(f32[128]{0:T(128)} %constant.34.clone) | copy-start | bytes 1540
  7.2 13.2 %copy-start = (f32[256,128]{1,0:T(8,128)S(1)}, f32[256,128]{1,0:T(8,128)}, u32[]{:S(2)}) copy-start(f32[256,128]{1,0:T(8,128)} %constant.35.clone.refs_11_.refs_2_) | copy-start | bytes 393220
  7.2 13.2 %copy-start.1 = (f32[256,128]{1,0:T(8,128)S(1)}, f32[256,128]{1,0:T(8,128)}, u32[]{:S(2)}) copy-start(f32[256,128]{1,0:T(8,128)} %constant.36.clone.refs_12_.refs_3_) | copy-start | bytes 393220
  7.3 13.2 %copy-start.3 = (f32[4,128]{1,0:T(4,128)S(1)}, f32[4,128]{1,0:T(4,128)}, u32[]{:S(2)}) copy-start(f32[4,128]{1,0:T(4,128)} %constant.37.clone.refs_13_.refs_4_) | copy-start | bytes 6148
  7.3 13.2 %copy-start.4 = (f32[4,128]{1,0:T(4,128)S(1)}, f32[4,128]{1,0:T(4,128)}, u32[]{:S(2)}) copy-start(f32[4,128]{1,0:T(4,128)} %constant.38.clone.refs_14_.refs_5_) | copy-start | bytes 6148
  7.3 13.2 %copy-start.5 = (bf16[2,2,256,128]{3,2,1,0:T(8,128)(2,1)S(1)}, bf16[2,2,256,128]{3,2,1,0:T(8,128)(2,1)}, u32[]{:S(2)}) copy-start(bf16[2,2,256,128]{3,2,1,0:T(8,128)(2,1)} %refs_0_.1) | copy-start | bytes 786436
  7.3 13.2 %copy-start.6 = (bf16[2,40,1024]{2,1,0:T(8,128)(2,1)S(1)}, bf16[2,40,1024]{2,1,0:T(8,128)(2,1)}, u32[]{:S(2)}) copy-start(bf16[2,40,1024]{2,1,0:T(8,128)(2,1)} %refs_7_.1) | copy-start | bytes 491524
  7.3 13.2 %copy-start.8 = (s32[4]{0:T(128)S(1)}, s32[4]{0:T(128)}, u32[]{:S(2)}) copy-start(s32[4]{0:T(128)} %length_ref.1) | copy-start | bytes 52
  7.3 5.5 %collective-permute-start.2 = (bf16[96,256]{1,0:T(8,128)(2,1)}, bf16[96,256]{1,0:T(8,128)(2,1)S(1)}, u32[]{:S(2)}, u32[]{:S(2)}) collective-permute-start(bf16[96,256]{1,0:T(8,128)(2,1)} %get-tuple-element.12), channel_id=1, source_target_pairs={{0,3},{1,2},{2,1},{3,0},{4,7},{5,6},{6,5},{7,4},{8,11},{9,10},{10,... | collective-permute-start | bytes 147464 | tf_op jit(solution)/shard_map/ppermute | solution.py:500
  8.0 4.8 %collective-permute-start.3 = (bf16[96,256]{1,0:T(8,128)(2,1)}, bf16[96,256]{1,0:T(8,128)(2,1)S(1)}, u32[]{:S(2)}, u32[]{:S(2)}) collective-permute-start(bf16[96,256]{1,0:T(8,128)(2,1)} %get-tuple-element.13), channel_id=1, source_target_pairs={{0,2},{1,3},{2,0},{3,1},{4,6},{5,7},{6,4},{7,5},{8,10},{9,11},{10,... | collective-permute-start | bytes 147464 | tf_op jit(solution)/shard_map/ppermute | solution.py:500
  11.4 1.5 %collective-permute-start.4 = (bf16[96,256]{1,0:T(8,128)(2,1)}, bf16[96,256]{1,0:T(8,128)(2,1)S(1)}, u32[]{:S(2)}, u32[]{:S(2)}) collective-permute-start(bf16[96,256]{1,0:T(8,128)(2,1)} %get-tuple-element.14), channel_id=1, source_target_pairs={{0,1},{1,0},{2,3},{3,2},{4,5},{5,4},{6,7},{7,6},{8,9},{9,8},{10,11... | collective-permute-start | bytes 147464 | tf_op jit(solution)/shard_map/ppermute | solution.py:500
  12.0 0.8 %copy-start.2 = (bf16[96,256]{1,0:T(8,128)(2,1)S(1)}, bf16[96,256]{1,0:T(8,128)(2,1)}, u32[]{:S(2)}) copy-start(bf16[96,256]{1,0:T(8,128)(2,1)} %get-tuple-element.15.value_ref) | copy-start | bytes 147460
  13.0 7.0 %collective-permute-start.6 = (bf16[2,2,48,128]{3,2,1,0:T(8,128)(2,1)S(1)}, bf16[2,2,48,128]{3,2,1,0:T(8,128)(2,1)S(1)}, u32[]{:S(2)}, u32[]{:S(2)}) collective-permute-start(bf16[2,2,48,128]{3,2,1,0:T(8,128)(2,1)S(1)} %finish.1.refs_3_.refs_6_.ahead_ref), channel_id=1, source_target_pairs={{0,8},{4,12},{8,0},{12,4},{1,9},{5,13},{9,1},{13,5},{2,10},{6,14},... | collective-permute-start | bytes 147464 | tf_op jit(solution)/shard_map/ppermute | solution.py:487
  16.0 4.4 %collective-permute-start.5 = (bf16[2,2,48,128]{3,2,1,0:T(8,128)(2,1)S(1)}, bf16[2,2,48,128]{3,2,1,0:T(8,128)(2,1)S(1)}, u32[]{:S(2)}, u32[]{:S(2)}) collective-permute-start(bf16[2,2,48,128]{3,2,1,0:T(8,128)(2,1)S(1)} %finish.1.refs_3_.refs_6_.ahead_ref), channel_id=1, source_target_pairs={{0,4},{4,0},{8,12},{12,8},{1,5},{5,1},{9,13},{13,9},{2,6},{6,2},{1... | collective-permute-start | bytes 147464 | tf_op jit(solution)/shard_map/ppermute | solution.py:487
  18.0 9.3 %collective-permute-start.7 = (bf16[2,2,256,128]{3,2,1,0:T(8,128)(2,1)S(1)}, bf16[2,2,256,128]{3,2,1,0:T(8,128)(2,1)S(1)}, u32[]{:S(2)}, u32[]{:S(2)}) collective-permute-start(bf16[2,2,256,128]{3,2,1,0:T(8,128)(2,1)S(1)} %assemble.1.refs_0_), channel_id=1, source_target_pairs={{0,4},{4,0},{8,12},{12,8},{1,5},{5,1},{9,13},{13,9},{2,6},{6,2},{1... | collective-permute-start | bytes 786440 | tf_op jit(solution)/shard_map/ppermute | solution.py:487
  20.0 7.2 %collective-permute-start.8 = (bf16[2,2,48,128]{3,2,1,0:T(8,128)(2,1)S(1)}, bf16[2,2,48,128]{3,2,1,0:T(8,128)(2,1)S(1)}, u32[]{:S(2)}, u32[]{:S(2)}) collective-permute-start(bf16[2,2,48,128]{3,2,1,0:T(8,128)(2,1)S(1)} %hold.3), channel_id=1, source_target_pairs={{0,4},{4,0},{8,12},{12,8},{1,5},{5,1},{9,13},{13,9},{2,6},{6,2},{1... | collective-permute-start | bytes 147464 | tf_op jit(solution)/shard_map/ppermute | solution.py:487
